TPU v7x, 32 devices: a whole 2x2x4 slice. The times are simulated.
32 devices in a mesh: seq: 8 (over z, x), ch: 4 (over y, core).
Axes of the slice: x: 2, y: 2, z: 4, core: 2. Of those that a mesh axis runs over, the one named last changes fastest.
Arguments:
- sequence: bfloat16 [4096, 4096], P('seq', 'ch'), may hold values from -6 to 6
- in_weight: bfloat16 [4096, 3, 4096], P(None, None, 'ch'), may hold values from -0.09375 to 0.09375
- short_weight: bfloat16 [7, 3, 4096], P(None, None, 'ch'), may hold values from -2.5 to 2.5
- filter_taps: bfloat16 [4096, 4096], P('seq', 'ch'), may hold values from -1 to 1
- out_weight: bfloat16 [4096, 4096], P('ch'), may hold values from -0.09375 to 0.09375
Outputs:
- result: bfloat16 [4096, 4096], P('seq', 'ch')
All inputs are finite; a program needn't handle non-finite values.
Results may differ from a plain program's by a relative error of at most 0.014.
Values may be sent and summed in bfloat16 or wider, within the bound.
No kernel may reach another device: no remote copies, remote signals or barrier semaphores. Data moves between devices by JAX's collectives and lax.ppermute only.
A program may use at most 192 MiB of HBM per device.

v0:
```python
import math

import jax
import jax.numpy as jnp
import numpy as np
from jax import lax
from jax.experimental import pallas as pl
from jax.experimental.pallas import tpu as pltpu
from jax.sharding import PartitionSpec as P

TAPS = 7
HALO = 16
bf16 = jnp.bfloat16
f32 = jnp.float32


def split_parts(table):
    high = table.astype(bf16)
    low = (table - high.astype(np.float64)).astype(bf16)
    return high, low


def fourier_tables(block):
    freqs = np.arange(block)[:, None] + 0.5
    spots = np.arange(block)[None, :]
    angle = 2.0 * math.pi * freqs * spots / (2 * block)
    forward = np.concatenate([np.cos(angle), -np.sin(angle)], 0)
    backward = np.concatenate([np.cos(angle).T, -np.sin(angle).T], 1) / block
    fwd_high, fwd_low = split_parts(forward)
    bwd_high, bwd_low = split_parts(backward)
    fwd = np.concatenate([fwd_high, fwd_low], 1)
    bwd = np.concatenate([bwd_high, bwd_low, bwd_high], 1)
    sign = np.broadcast_to(np.where(np.arange(8) % 2 == 0, 1.0, -1.0)[:, None], (8, 128))
    return fwd, bwd, sign.astype(np.float32)


def swap(shard, axis, bit):
    size = lax.axis_size(axis)
    return lax.ppermute(shard, axis, [(i, i ^ bit) for i in range(size)])


def vmem_spec():
    return pl.BlockSpec(memory_space=pltpu.VMEM)


def params(mib):
    return pltpu.CompilerParams(vmem_limit_bytes=mib * 1024 * 1024)


def cost(flops, moved):
    return pl.CostEstimate(flops=flops, bytes_accessed=moved, transcendentals=0)


def project_kernel(pieces, strip, own_ref, *refs):
    x_refs = refs[:pieces]
    w_refs = refs[pieces : 2 * pieces]
    tap_ref, query_ref, product_ref, ext_ref = refs[2 * pieces :]
    rows, width = query_ref.shape
    for branch in range(3):
        total = None
        for x_ref, w_ref in zip(x_refs, w_refs):
            term = jnp.dot(x_ref[...], w_ref[branch], preferred_element_type=f32)
            total = term if total is None else total + term
        ext_ref[branch] = total.astype(bf16).astype(f32)
    step = 64
    for lane in range(0, width, strip):
        lanes = slice(lane, lane + strip)
        for row in range(0, rows, step):

            def mixed(branch):
                running = None
                for offset in range(TAPS):
                    lead = row + HALO - offset
                    term = tap_ref[branch, offset : offset + 1, lanes] * ext_ref[branch, lead : lead + step, lanes]
                    running = term if running is None else running + term
                return running.astype(bf16)

            here = slice(row, row + step)
            query_ref[here, lanes] = mixed(0)
            product = (mixed(1).astype(f32) * mixed(2).astype(f32)).astype(bf16)
            if len(product_ref.shape) == 3:
                product_ref[lane // strip, here, :] = product
            else:
                product_ref[here, lanes] = product


def project(own, pieces, weights, tap_table, blocks):
    count = len(pieces)
    rows_in, depth = pieces[0].shape
    rows = rows_in - HALO
    width = weights.shape[2]
    tile = 256
    chan = width // blocks
    direct = chan % 128 == 0 and tile % chan == 0
    strip = chan if direct else 128
    if direct:
        product_shape = (blocks, rows, chan)
        product_spec = pl.BlockSpec((tile // chan, rows, chan), lambda i, own: (i, 0, 0))
    else:
        product_shape = (rows, width)
        product_spec = pl.BlockSpec((rows, tile), lambda i, own: (0, i))

    def weight_spec(p):
        return pl.BlockSpec((3, depth, tile), lambda i, own: (0, own[0] ^ p, i))

    query, product = pl.pallas_call(
        lambda *refs: project_kernel(count, strip, *refs),
        grid_spec=pltpu.PrefetchScalarGridSpec(
            num_scalar_prefetch=1,
            grid=(width // tile,),
            in_specs=[vmem_spec()] * count
            + [weight_spec(p) for p in range(count)]
            + [pl.BlockSpec((3, TAPS, tile), lambda i, own: (0, 0, i))],
            out_specs=[pl.BlockSpec((rows, tile), lambda i, own: (0, i)), product_spec],
            scratch_shapes=[pltpu.VMEM((3, rows_in, tile), f32)],
        ),
        out_shape=[
            jax.ShapeDtypeStruct((rows, width), bf16),
            jax.ShapeDtypeStruct(product_shape, bf16),
        ],
        compiler_params=params(32),
        cost_estimate=cost(2 * rows_in * count * depth * 3 * width, 6 * count * depth * width),
        name="project",
    )(own, *pieces, *([weights] * count), tap_table)
    if not direct:
        product = product.reshape(rows, blocks, chan).transpose(1, 0, 2)
    return query, product


def transform_into(fwd_ref, in_ref, picks, out_ref, places):
    block, chan = in_ref.shape[1:]
    group = 2 if chan % 128 == 0 and len(picks) % 2 == 0 else 1
    for start in range(0, len(picks), group):
        signal = jnp.concatenate([in_ref[k] for k in picks[start : start + group]], 1)
        stacked = jnp.concatenate([signal, signal], 0)
        result = jnp.dot(fwd_ref[...], stacked, preferred_element_type=f32)
        for j in range(group):
            lanes = slice(j * chan, (j + 1) * chan)
            out_ref[0, places[start + j]] = result[:block, lanes]
            out_ref[1, places[start + j]] = result[block:, lanes]


def filter_kernel(fwd_ref, sign_ref, taps_ref, out_ref, spec_ref):
    count, block, chan = taps_ref.shape
    transform_into(fwd_ref, taps_ref, range(count), spec_ref, range(count))
    sign = sign_ref[:, :chan]

    def body(i, carry):
        rows = pl.ds(pl.multiple_of(i * 8, 8), 8)
        prev = None
        for k in range(count):
            real, imag = spec_ref[0, k, rows, :], spec_ref[1, k, rows, :]
            if prev is None:
                out_ref[0, k, rows, :] = real
                out_ref[1, k, rows, :] = imag
            else:
                out_ref[0, k, rows, :] = real - sign * prev[1]
                out_ref[1, k, rows, :] = imag + sign * prev[0]
            prev = (real, imag)
        return carry

    lax.fori_loop(0, block // 8, body, 0)


def filter_spectra(fwd, sign, taps):
    count, block, chan = taps.shape
    shape = (2, count, block, chan)
    return pl.pallas_call(
        filter_kernel,
        in_specs=[vmem_spec()] * 3,
        out_specs=vmem_spec(),
        out_shape=jax.ShapeDtypeStruct(shape, f32),
        scratch_shapes=[pltpu.VMEM(shape, f32)],
        compiler_params=params(32),
        cost_estimate=cost(2 * 2 * count * chan * 4 * block * block, 8 * count * block * chan),
        name="filter_spectra",
    )(fwd, sign, taps)


def accumulate(filt_ref, spec_ref, sources, init_ref, targets, write):
    block = filt_ref.shape[2]

    def body(i, carry):
        rows = pl.ds(pl.multiple_of(i * 8, 8), 8)
        for place, target in enumerate(targets):
            real = imag = None
            if init_ref is not None:
                real, imag = init_ref[0, place, rows, :], init_ref[1, place, rows, :]
            for slot, source in enumerate(sources):
                if source > target:
                    continue
                lag = target - source
                xr, xi = spec_ref[0, slot, rows, :], spec_ref[1, slot, rows, :]
                gr, gi = filt_ref[0, lag, rows, :], filt_ref[1, lag, rows, :]
                if real is None:
                    real, imag = xr * gr - xi * gi, xr * gi + xi * gr
                else:
                    real = real + xr * gr - xi * gi
                    imag = imag + xr * gi + xi * gr
            if real is None:
                real = imag = jnp.zeros((8, filt_ref.shape[3]), f32)
            write(rows, place, real, imag)
        return carry

    lax.fori_loop(0, block // 8, body, 0)


def inverse_into(bwd_ref, sum_ref, out_ref):
    count, double, chan = sum_ref.shape
    group = 2 if chan % 128 == 0 and count % 2 == 0 else 1
    for start in range(0, count, group):
        full = jnp.concatenate([sum_ref[start + j] for j in range(group)], 1)
        high = full.astype(bf16)
        low = (full - high.astype(f32)).astype(bf16)
        stacked = jnp.concatenate([high, high, low], 0)
        result = jnp.dot(bwd_ref[...], stacked, preferred_element_type=f32).astype(out_ref.dtype)
        for j in range(group):
            out_ref[start + j] = result[:, j * chan : (j + 1) * chan]


def early_kernel(fwd_ref, filt_ref, half_ref, same_ref, other_ref, spec_ref):
    half = half_ref.shape[0]
    odd, even = [2 * k + 1 for k in range(half)], [2 * k for k in range(half)]
    transform_into(fwd_ref, half_ref, range(half), spec_ref, range(half))

    def to(ref):
        def write(rows, place, real, imag):
            ref[0, place, rows, :] = real
            ref[1, place, rows, :] = imag

        return write

    accumulate(filt_ref, spec_ref, odd, None, odd, to(same_ref))
    accumulate(filt_ref, spec_ref, odd, None, even, to(other_ref))


def write_sums(sum_ref, block):
    def write(rows, place, real, imag):
        sum_ref[place, rows, :] = real
        sum_ref[place, pl.ds(rows.start + block, 8), :] = imag

    return write


def middle_kernel(fwd_ref, bwd_ref, filt_ref, half_ref, init_ref, out_ref, spec_ref, sum_ref):
    half, block, _ = half_ref.shape
    even = [2 * k for k in range(half)]
    transform_into(fwd_ref, half_ref, range(half), spec_ref, range(half))
    accumulate(filt_ref, spec_ref, even, init_ref, even, write_sums(sum_ref, block))
    inverse_into(bwd_ref, sum_ref, out_ref)


def late_kernel(bwd_ref, filt_ref, spec_ref, init_ref, out_ref, sum_ref):
    _, half, block, _ = spec_ref.shape
    odd, even = [2 * k + 1 for k in range(half)], [2 * k for k in range(half)]
    accumulate(filt_ref, spec_ref, even, init_ref, odd, write_sums(sum_ref, block))
    inverse_into(bwd_ref, sum_ref, out_ref)


def early(fwd, filt, part):
    half, block, chan = part.shape
    spec = jax.ShapeDtypeStruct((2, half, block, chan), f32)
    return pl.pallas_call(
        early_kernel,
        in_specs=[vmem_spec()] * 3,
        out_specs=[vmem_spec()] * 2,
        out_shape=[spec, spec],
        scratch_shapes=[pltpu.VMEM(spec.shape, f32)],
        compiler_params=params(32),
        cost_estimate=cost(2 * half * chan * 4 * block * block * 2, 32 * half * block * chan),
        name="early_blocks",
    )(fwd, filt, part)


def middle(fwd, bwd, filt, part, init):
    half, block, chan = part.shape
    spec = jax.ShapeDtypeStruct((2, half, block, chan), f32)
    return pl.pallas_call(
        middle_kernel,
        in_specs=[vmem_spec()] * 5,
        out_specs=[vmem_spec()] * 2,
        out_shape=[jax.ShapeDtypeStruct(part.shape, bf16), spec],
        scratch_shapes=[pltpu.VMEM((half, 2 * block, chan), f32)],
        compiler_params=params(32),
        cost_estimate=cost(2 * half * chan * 10 * block * block * 2, 32 * half * block * chan),
        name="middle_blocks",
    )(fwd, bwd, filt, part, init)


def late(bwd, filt, spec, init):
    _, half, block, chan = spec.shape
    return pl.pallas_call(
        late_kernel,
        in_specs=[vmem_spec()] * 4,
        out_specs=vmem_spec(),
        out_shape=jax.ShapeDtypeStruct((half, block, chan), bf16),
        scratch_shapes=[pltpu.VMEM((half, 2 * block, chan), f32)],
        compiler_params=params(32),
        cost_estimate=cost(2 * half * chan * 6 * block * block * 2, 32 * half * block * chan),
        name="late_blocks",
    )(bwd, filt, spec, init)


def output_kernel(own_ref, query_ref, conv_ref, w_ref, out_ref, gated_ref):
    blocks, _, chan = conv_ref.shape

    @pl.when((pl.program_id(0) == 0) & (pl.program_id(1) == 0))
    def _():
        for k in range(blocks):
            lanes = slice(k * chan, (k + 1) * chan)
            gated_ref[:, lanes] = (query_ref[:, lanes].astype(f32) * conv_ref[k].astype(f32)).astype(bf16)

    out_ref[0] = jnp.dot(gated_ref[...], w_ref[...], preferred_element_type=f32).astype(bf16)


def output_terms(own, query, conv, weights, parts):
    rows, width = query.shape
    wide = weights.shape[1] // parts
    tile = 512
    tiles = wide // tile
    return pl.pallas_call(
        output_kernel,
        grid_spec=pltpu.PrefetchScalarGridSpec(
            num_scalar_prefetch=1,
            grid=(parts, tiles),
            in_specs=[
                vmem_spec(),
                vmem_spec(),
                pl.BlockSpec((width, tile), lambda p, i, own: (0, (own[0] ^ p) * tiles + i)),
            ],
            out_specs=pl.BlockSpec((1, rows, tile), lambda p, i, own: (p, 0, i)),
            scratch_shapes=[pltpu.VMEM((rows, width), bf16)],
        ),
        out_shape=jax.ShapeDtypeStruct((parts, rows, wide), bf16),
        compiler_params=params(24),
        cost_estimate=cost(2 * rows * width * parts * wide, 2 * width * parts * wide),
        name="output_terms",
    )(own, query, conv, weights)


def body(sequence, in_weight, short_weight, filter_taps, out_weight):
    rows, width = sequence.shape
    blocks = lax.axis_size("seq")
    parts = lax.axis_size("ch")
    chan = width // blocks
    block = rows // 2
    fwd, bwd, sign = fourier_tables(block)
    own = lax.axis_index("ch").astype(jnp.int32).reshape(1)
    weights = in_weight.transpose(1, 0, 2)
    tap_table = short_weight.astype(f32).transpose(1, 0, 2)
    bits = [1 << k for k in range(parts.bit_length() - 1)]

    def exchange(values):
        return lax.all_to_all(values, "seq", split_axis=0, concat_axis=0, tiled=True)

    taps = exchange(filter_taps.reshape(rows, blocks, chan).transpose(1, 0, 2))
    border = lax.ppermute(sequence[rows - HALO :], "seq", [(i, i + 1) for i in range(blocks - 1)])
    late_rows = sequence[block - HALO :]
    early_rows = jnp.concatenate([border, sequence[:block]], 0)

    def gather(shard):
        pieces = {0: shard}
        for bit in bits[1:] + bits[:1]:
            pieces.update({p | bit: swap(piece, "ch", bit) for p, piece in pieces.items()})
        return [pieces[p] for p in range(parts)]

    filt = filter_spectra(fwd, sign, taps.reshape(2 * blocks, block, chan))
    query_odd, product_odd = project(own, gather(late_rows), weights, tap_table, blocks)
    product_odd = exchange(product_odd)
    query_even, product_even = project(own, gather(early_rows), weights, tap_table, blocks)
    product_even = exchange(product_even)
    init_odd, init_even = early(fwd, filt, product_odd)
    conv_even, spec_even = middle(fwd, bwd, filt, product_even, init_even)
    conv_even = exchange(conv_even)
    conv_odd = late(bwd, filt, spec_even, init_odd)
    conv_odd = exchange(conv_odd)

    def finish(query, conv):
        terms = output_terms(own, query, conv, out_weight, parts)
        held = {p: terms[p] for p in range(parts)}
        for bit in bits:
            arrived = {p ^ bit: swap(held[p], "ch", bit) for p in held if p & bit}
            held = {p: (held[p].astype(f32) + arrived[p].astype(f32)).astype(bf16) for p in arrived}
        return held[0]

    return jnp.concatenate([finish(query_even, conv_even), finish(query_odd, conv_odd)], 0)


def solution(mesh):
    return jax.shard_map(
        body,
        mesh=mesh,
        in_specs=(
            P("seq", "ch"),
            P(None, None, "ch"),
            P(None, None, "ch"),
            P("seq", "ch"),
            P("ch", None),
        ),
        out_specs=P("seq", "ch"),
        check_vma=False,
    )
```

profile of v0, /device:TPU:0, one launch (start us, length us, event | category | flops | bytes accessed | tf_op | source)
XLA Modules:
  0.0 192.5 jit_solution(17632645322125736408)
XLA Ops:
  0.0 1.2 copy-done
  1.2 1.2 bitcast_bitcast_fusion
  2.4 7.3 %all-to-all-start = ((bf16[8,512,128]{2,1,0:T(8,128)(2,1)}), bf16[8,512,128]{2,1,0:T(8,128)(2,1)S(1)}, u32[]{:S(2)}, u32[]{:S(2)}) async-start(bf16[8,512,128]{2,1,0:T(8,128)(2,1)} %bitcast_bitcast_fusion), calls=%async_computation | async-start | bytes 2097152 | tf_op jit(solution)/shard_map/all_to_all | solution.py:354
  9.7 1.6 collective-permute-start.5
  11.3 3.9 %collective-permute-start = (bf16[16,1024]{1,0:T(8,128)(2,1)S(1)}, bf16[16,1024]{1,0:T(8,128)(2,1)S(1)}, u32[]{:S(2)}, u32[]{:S(2)}) collective-permute-start(bf16[16,1024]{1,0:T(8,128)(2,1)S(1)} %slice.33), channel_id=1, source_target_pairs={{0,4},{4,8},{8,12},{12,16},{16,20},{20,24},{24,28},{1,5},{5,9},{9,... | collective-permute-start | bytes 98312 | tf_op jit(solution)/shard_map/ppermute | solution.py:357
  15.2 2.6 %collective-permute-done = bf16[16,1024]{1,0:T(8,128)(2,1)S(1)} collective-permute-done((bf16[16,1024]{1,0:T(8,128)(2,1)S(1)}, bf16[16,1024]{1,0:T(8,128)(2,1)S(1)}, u32[]{:S(2)}, u32[]{:S(2)}) %collective-permute-start) | collective-permute-done | bytes 32800 | tf_op jit(solution)/shard_map/ppermute | solution.py:357
  17.9 1.6 collective-permute-start.2
  19.5 6.0 %collective-permute-done.5.refs_3_ = bf16[272,1024]{1,0:T(8,128)(2,1)} collective-permute-done((bf16[272,1024]{1,0:T(8,128)(2,1)S(1)}, bf16[272,1024]{1,0:T(8,128)(2,1)}, u32[]{:S(2)}, u32[]{:S(2)}) %collective-permute-start.5) | collective-permute-done | bytes 557088 | tf_op jit(solution)/shard_map/ppermute | solution.py:39
  26.0 9.8 %collective-permute-done.2.refs_3_ = bf16[272,1024]{1,0:T(8,128)(2,1)S(1)} collective-permute-done((bf16[272,1024]{1,0:T(8,128)(2,1)S(1)}, bf16[272,1024]{1,0:T(8,128)(2,1)S(1)}, u32[]{:S(2)}, u32[]{:S(2)}) %collective-permute-start.2) | collective-permute-done | bytes 557088 | tf_op jit(solution)/shard_map/ppermute | solution.py:39
  35.8 14.5 %project.3 = (bf16[256,1024]{1,0:T(8,128)(2,1)S(1)}, bf16[8,256,128]{2,1,0:T(8,128)(2,1)S(1)}) custom-call(s32[1]{0:T(128)} %bitcast.refs_0_.own_ref, bf16[272,1024]{1,0:T(8,128)(2,1)S(1)} %slice.35.refs_1_, bf16[272,1024]{1,0:T(8,128)(2,1)} %collective-permute-done.4.refs_2_, bf16[272,1024]{1,0:T(8,128)(2,1)} %collective-permute-done.5.refs_3_, ...), custom_call_target="tpu_custom_call" | custom-call | flops 6845104128 | bytes 25165824 | tf_op jit(solution)/shard_map/project/pallas_call | solution.py:106
  51.1 0.8 copy-done.20
  51.9 1.0 copy-done.11
  52.9 17.7 %all-to-all-start.2 = ((bf16[8,256,128]{2,1,0:T(8,128)(2,1)}), bf16[8,256,128]{2,1,0:T(8,128)(2,1)S(1)}, u32[]{:S(2)}, u32[]{:S(2)}) async-start(bf16[8,256,128]{2,1,0:T(8,128)(2,1)} %copy-done.20), calls=%async_computation.2 | async-start | bytes 1048576 | tf_op jit(solution)/shard_map/all_to_all | solution.py:354
  70.6 14.4 %project.2 = (bf16[256,1024]{1,0:T(8,128)(2,1)S(1)}, bf16[8,256,128]{2,1,0:T(8,128)(2,1)S(1)}) custom-call(s32[1]{0:T(128)} %bitcast.refs_0_.own_ref, bf16[272,1024]{1,0:T(8,128)(2,1)S(1)} %pad_maximum_fusion.1.refs_1_, bf16[272,1024]{1,0:T(8,128)(2,1)} %collective-permute-done.1.refs_2_, bf16[272,1024]{1,0:T(8,128)(2,1)S(1)} %collective-permute-done.2.refs_3_, ...), custom_call_target="tpu_custom_call" | custom-call | flops 6845104128 | bytes 25165824 | tf_op jit(solution)/shard_map/project/pallas_call | solution.py:106
  85.8 0.9 copy-done.21
  86.6 6.0 %all-to-all-start.1 = ((bf16[8,256,128]{2,1,0:T(8,128)(2,1)}), bf16[8,256,128]{2,1,0:T(8,128)(2,1)}, u32[]{:S(2)}, u32[]{:S(2)}) async-start(bf16[8,256,128]{2,1,0:T(8,128)(2,1)} %copy-done.21), calls=%async_computation.1 | async-start | bytes 1048576 | tf_op jit(solution)/shard_map/all_to_all | solution.py:354
  92.6 1.0 copy-done.14
  93.7 2.1 %filter_spectra.1.filt_ref = f32[2,16,256,128]{3,2,1,0:T(8,128)S(1)} custom-call(bf16[512,512]{1,0:T(8,128)(2,1)S(1)} %copy-done.14, f32[8,128]{1,0:T(8,128)S(1)} %copy-done.25, bf16[16,256,128]{2,1,0:T(8,128)(2,1)S(1)} %bitcast.40), custom_call_target="tpu_custom_call" | custom-call | flops 2147483648 | bytes 4194304 | tf_op jit(solution)/shard_map/filter_spectra/pallas_call | solution.py:168
  95.8 3.5 %early_blocks.1 = (f32[2,8,256,128]{3,2,1,0:T(8,128)S(1)}, f32[2,8,256,128]{3,2,1,0:T(8,128)S(1)}) custom-call(bf16[512,512]{1,0:T(8,128)(2,1)S(1)} %copy-done.14, f32[2,16,256,128]{3,2,1,0:T(8,128)S(1)} %filter_spectra.1.filt_ref, bf16[8,256,128]{2,1,0:T(8,128)(2,1)S(1)} %all-to-all-done.2.half_ref), custom_call_target="tpu_custom_call" | custom-call | flops 1073741824 | bytes 8388608 | tf_op jit(solution)/shard_map/early_blocks/pallas_call | solution.py:263
  99.3 2.0 %copy-done.4 = f32[2,16,256,128]{3,2,1,0:T(8,128)} copy-done((f32[2,16,256,128]{3,2,1,0:T(8,128)}, f32[2,16,256,128]{3,2,1,0:T(8,128)S(1)}, u32[]{:S(2)}) %copy-start.4) | copy-done | bytes 4194328
  101.3 1.3 copy-done.23
  102.7 4.7 %all-to-all-done.1.half_ref = bf16[8,256,128]{2,1,0:T(8,128)(2,1)} async-done(((bf16[8,256,128]{2,1,0:T(8,128)(2,1)}), bf16[8,256,128]{2,1,0:T(8,128)(2,1)}, u32[]{:S(2)}, u32[]{:S(2)}) %all-to-all-start.1) | async-done | bytes 524320 | tf_op jit(solution)/shard_map/all_to_all | solution.py:354
  107.3 2.2 %copy-done.5 = f32[2,16,256,128]{3,2,1,0:T(8,128)S(1)} copy-done((f32[2,16,256,128]{3,2,1,0:T(8,128)S(1)}, f32[2,16,256,128]{3,2,1,0:T(8,128)}, u32[]{:S(2)}) %copy-start.5) | copy-done | bytes 4194328
  109.5 1.0 copy-done.15
  110.5 1.6 copy-done.24
  112.1 4.4 %middle_blocks.1 = (bf16[8,256,128]{2,1,0:T(8,128)(2,1)S(1)}, f32[2,8,256,128]{3,2,1,0:T(8,128)S(1)}) custom-call(bf16[512,512]{1,0:T(8,128)(2,1)S(1)} %copy-done.15, bf16[256,1536]{1,0:T(8,128)(2,1)S(1)} %copy-done.13, f32[2,16,256,128]{3,2,1,0:T(8,128)S(1)} %copy-done.5, bf16[8,256,128]{2,1,0:T(8,128)(2,1)} %all-to-all-done.1.half_ref, ...), custom_call_target="tpu_custom_call" | custom-call | flops 2684354560 | bytes 8388608 | tf_op jit(solution)/shard_map/middle_blocks/pallas_call | solution.py:278
  116.5 1.3 copy-done.7
  117.9 0.8 copy-done.22
  118.7 3.6 %all-to-all-start.3 = ((bf16[8,256,128]{2,1,0:T(8,128)(2,1)}), bf16[8,256,128]{2,1,0:T(8,128)(2,1)S(1)}, u32[]{:S(2)}, u32[]{:S(2)}) async-start(bf16[8,256,128]{2,1,0:T(8,128)(2,1)} %copy-done.22), calls=%async_computation.3 | async-start | bytes 1048576 | tf_op jit(solution)/shard_map/all_to_all | solution.py:354
  122.4 2.2 %copy-done.6 = f32[2,16,256,128]{3,2,1,0:T(8,128)S(1)} copy-done((f32[2,16,256,128]{3,2,1,0:T(8,128)S(1)}, f32[2,16,256,128]{3,2,1,0:T(8,128)}, u32[]{:S(2)}) %copy-start.6) | copy-done | bytes 4194328
  124.6 1.6 copy-done.8
  126.1 3.5 %late_blocks.1 = bf16[8,256,128]{2,1,0:T(8,128)(2,1)} custom-call(bf16[256,1536]{1,0:T(8,128)(2,1)S(1)} %copy-done.13, f32[2,16,256,128]{3,2,1,0:T(8,128)S(1)} %copy-done.6, f32[2,8,256,128]{3,2,1,0:T(8,128)S(1)} %copy-done.8, f32[2,8,256,128]{3,2,1,0:T(8,128)S(1)} %get-tuple-element.20.init_ref), custom_call_target="tpu_custom_call" | custom-call | flops 1610612736 | bytes 8388608 | tf_op jit(solution)/shard_map/late_blocks/pallas_call | solution.py:292
  129.6 7.4 %all-to-all-done.3.conv_ref = bf16[8,256,128]{2,1,0:T(8,128)(2,1)S(1)} async-done(((bf16[8,256,128]{2,1,0:T(8,128)(2,1)}), bf16[8,256,128]{2,1,0:T(8,128)(2,1)S(1)}, u32[]{:S(2)}, u32[]{:S(2)}) %all-to-all-start.3) | async-done | bytes 524320 | tf_op jit(solution)/shard_map/all_to_all | solution.py:354
  137.0 3.7 %all-to-all-start.4 = ((bf16[8,256,128]{2,1,0:T(8,128)(2,1)}), bf16[8,256,128]{2,1,0:T(8,128)(2,1)S(1)}, u32[]{:S(2)}, u32[]{:S(2)}) async-start(bf16[8,256,128]{2,1,0:T(8,128)(2,1)} %late_blocks.1), calls=%async_computation.4 | async-start | bytes 1048576 | tf_op jit(solution)/shard_map/all_to_all | solution.py:354
  140.7 3.4 %copy-done.2 = bf16[1024,4096]{1,0:T(8,128)(2,1)S(1)} copy-done((bf16[1024,4096]{1,0:T(8,128)(2,1)S(1)}, bf16[1024,4096]{1,0:T(8,128)(2,1)}, u32[]{:S(2)}) %copy-start.2) | copy-done | bytes 8388632
  144.1 1.0 copy-done.10
  145.2 1.0 copy-done.19
  146.2 4.5 %output_terms.2 = bf16[4,256,1024]{2,1,0:T(8,128)(2,1)S(1)} custom-call(s32[1]{0:T(128)} %bitcast.refs_0_.own_ref, bf16[256,1024]{1,0:T(8,128)(2,1)S(1)} %copy-done.19, bf16[8,256,128]{2,1,0:T(8,128)(2,1)S(1)} %copy-done.10, bf16[1024,4096]{1,0:T(8,128)(2,1)S(1)} %copy-done.2), custom_call_target="tpu_custom_call" | custom-call | flops 2147483648 | bytes 8388608 | tf_op jit(solution)/shard_map/output_terms/pallas_call | solution.py:321
  150.7 1.1 slice_bitcast_fusion.6
  151.8 3.5 %all-to-all-done.4.conv_ref = bf16[8,256,128]{2,1,0:T(8,128)(2,1)S(1)} async-done(((bf16[8,256,128]{2,1,0:T(8,128)(2,1)}), bf16[8,256,128]{2,1,0:T(8,128)(2,1)S(1)}, u32[]{:S(2)}, u32[]{:S(2)}) %all-to-all-start.4) | async-done | bytes 524320 | tf_op jit(solution)/shard_map/all_to_all | solution.py:354
  155.3 3.4 %copy-done.3 = bf16[1024,4096]{1,0:T(8,128)(2,1)S(1)} copy-done((bf16[1024,4096]{1,0:T(8,128)(2,1)S(1)}, bf16[1024,4096]{1,0:T(8,128)(2,1)}, u32[]{:S(2)}) %copy-start.3) | copy-done | bytes 8388632
  158.7 4.5 %output_terms.3 = bf16[4,256,1024]{2,1,0:T(8,128)(2,1)S(1)} custom-call(s32[1]{0:T(128)} %bitcast.refs_0_.own_ref, bf16[256,1024]{1,0:T(8,128)(2,1)S(1)} %copy-done.17, bf16[8,256,128]{2,1,0:T(8,128)(2,1)S(1)} %all-to-all-done.4.conv_ref, bf16[1024,4096]{1,0:T(8,128)(2,1)S(1)} %copy-done.3), custom_call_target="tpu_custom_call" | custom-call | flops 2147483648 | bytes 8388608 | tf_op jit(solution)/shard_map/output_terms/pallas_call | solution.py:321
  163.4 0.9 copy-done.27
  164.3 1.2 fusion.2
  165.5 1.6 collective-permute-start.9
  168.1 12.2 %collective-permute-done.9 = bf16[256,1024]{1,0:T(8,128)(2,1)S(1)} collective-permute-done((bf16[256,1024]{1,0:T(8,128)(2,1)S(1)}, bf16[256,1024]{1,0:T(8,128)(2,1)S(1)}, u32[]{:S(2)}, u32[]{:S(2)}) %collective-permute-start.9) | collective-permute-done | bytes 524320 | tf_op jit(solution)/shard_map/ppermute | solution.py:39
  180.6 10.6 %collective-permute-done.12 = bf16[256,1024]{1,0:T(8,128)(2,1)S(1)} collective-permute-done((bf16[256,1024]{1,0:T(8,128)(2,1)S(1)}, bf16[256,1024]{1,0:T(8,128)(2,1)S(1)}, u32[]{:S(2)}, u32[]{:S(2)}) %collective-permute-start.12) | collective-permute-done | bytes 524320 | tf_op jit(solution)/shard_map/ppermute | solution.py:39
  191.5 1.0 pad_maximum_fusion
  (68 shorter events, 4.0 us)
Async XLA Ops:
  0.0 1.2 copy-start
  0.0 9.6 %copy-start.26 = (bf16[512,1024]{1,0:T(8,128)(2,1)S(1)}, bf16[512,1024]{1,0:T(8,128)(2,1)}, u32[]{:S(2)}) copy-start(bf16[512,1024]{1,0:T(8,128)(2,1)} %param.8) | copy-start | bytes 3145732
  2.4 49.5 %all-to-all-start = ((bf16[8,512,128]{2,1,0:T(8,128)(2,1)}), bf16[8,512,128]{2,1,0:T(8,128)(2,1)S(1)}, u32[]{:S(2)}, u32[]{:S(2)}) async-start(bf16[8,512,128]{2,1,0:T(8,128)(2,1)} %bitcast_bitcast_fusion), calls=%async_computation | async-start | bytes 2097152 | tf_op jit(solution)/shard_map/all_to_all | solution.py:354
  9.6 8.2 %slice-start = ((bf16[512,1024]{1,0:T(8,128)(2,1)}), bf16[256,1024]{1,0:T(8,128)(2,1)S(1)}, s32[]{:S(2)}) async-start(bf16[512,1024]{1,0:T(8,128)(2,1)} %param.8), calls=%async_computation.5 | async-start | bytes 1048576 | tf_op jit(solution)/shard_map/slice | solution.py:359
  9.7 15.8 %copy-start.28 = (bf16[7,3,1024]{2,0,1:T(8,128)(2,1)S(1)}, bf16[7,3,1024]{2,0,1:T(8,128)(2,1)}, u32[]{:S(2)}) copy-start(bf16[7,3,1024]{2,0,1:T(8,128)(2,1)} %param.10) | copy-start | bytes 129028
  9.7 15.7 %collective-permute-start.5 = (bf16[272,1024]{1,0:T(8,128)(2,1)S(1)}, bf16[272,1024]{1,0:T(8,128)(2,1)}, u32[]{:S(2)}, u32[]{:S(2)}) collective-permute-start(bf16[272,1024]{1,0:T(8,128)(2,1)S(1)} %slice.35.refs_1_), channel_id=1, source_target_pairs={{0,2},{1,3},{2,0},{3,1},{4,6},{5,7},{6,4},{7,5},{8,10},{9,11},{10,... | collective-permute-start | bytes 1671176 | tf_op jit(solution)/shard_map/ppermute | solution.py:39
  11.3 6.5 %collective-permute-start = (bf16[16,1024]{1,0:T(8,128)(2,1)S(1)}, bf16[16,1024]{1,0:T(8,128)(2,1)S(1)}, u32[]{:S(2)}, u32[]{:S(2)}) collective-permute-start(bf16[16,1024]{1,0:T(8,128)(2,1)S(1)} %slice.33), channel_id=1, source_target_pairs={{0,4},{4,8},{8,12},{12,16},{16,20},{20,24},{24,28},{1,5},{5,9},{9,... | collective-permute-start | bytes 98312 | tf_op jit(solution)/shard_map/ppermute | solution.py:357
  17.9 17.9 %collective-permute-start.2 = (bf16[272,1024]{1,0:T(8,128)(2,1)S(1)}, bf16[272,1024]{1,0:T(8,128)(2,1)S(1)}, u32[]{:S(2)}, u32[]{:S(2)}) collective-permute-start(bf16[272,1024]{1,0:T(8,128)(2,1)S(1)} %pad_maximum_fusion.1.refs_1_), channel_id=1, source_target_pairs={{0,2},{1,3},{2,0},{3,1},{4,6},{5,7},{6,4},{7,5},{8,10},{9,11},{10,... | collective-permute-start | bytes 1671176 | tf_op jit(solution)/shard_map/ppermute | solution.py:39
  19.5 16.3 %collective-permute-start.4 = (bf16[272,1024]{1,0:T(8,128)(2,1)S(1)}, bf16[272,1024]{1,0:T(8,128)(2,1)}, u32[]{:S(2)}, u32[]{:S(2)}) collective-permute-start(bf16[272,1024]{1,0:T(8,128)(2,1)S(1)} %slice.35.refs_1_), channel_id=1, source_target_pairs={{0,1},{1,0},{2,3},{3,2},{4,5},{5,4},{6,7},{7,6},{8,9},{9,8},{10,11... | collective-permute-start | bytes 1671176 | tf_op jit(solution)/shard_map/ppermute | solution.py:39
  25.4 10.4 %collective-permute-start.6 = (bf16[272,1024]{1,0:T(8,128)(2,1)}, bf16[272,1024]{1,0:T(8,128)(2,1)}, u32[]{:S(2)}, u32[]{:S(2)}) collective-permute-start(bf16[272,1024]{1,0:T(8,128)(2,1)} %collective-permute-done.5.refs_3_), channel_id=1, source_target_pairs={{0,1},{1,0},{2,3},{3,2},{4,5},{5,4},{6,7},{7,6},{8,9},{9,8},{10,11... | collective-permute-start | bytes 1671176 | tf_op jit(solution)/shard_map/ppermute | solution.py:39
  25.5 45.1 %collective-permute-start.1 = (bf16[272,1024]{1,0:T(8,128)(2,1)S(1)}, bf16[272,1024]{1,0:T(8,128)(2,1)}, u32[]{:S(2)}, u32[]{:S(2)}) collective-permute-start(bf16[272,1024]{1,0:T(8,128)(2,1)S(1)} %pad_maximum_fusion.1.refs_1_), channel_id=1, source_target_pairs={{0,1},{1,0},{2,3},{3,2},{4,5},{5,4},{6,7},{7,6},{8,9},{9,8},{10,11... | collective-permute-start | bytes 1671176 | tf_op jit(solution)/shard_map/ppermute | solution.py:39
  35.8 34.8 %collective-permute-start.3 = (bf16[272,1024]{1,0:T(8,128)(2,1)S(1)}, bf16[272,1024]{1,0:T(8,128)(2,1)}, u32[]{:S(2)}, u32[]{:S(2)}) collective-permute-start(bf16[272,1024]{1,0:T(8,128)(2,1)S(1)} %collective-permute-done.2.refs_3_), channel_id=1, source_target_pairs={{0,1},{1,0},{2,3},{3,2},{4,5},{5,4},{6,7},{7,6},{8,9},{9,8},{10,11... | collective-permute-start | bytes 1671176 | tf_op jit(solution)/shard_map/ppermute | solution.py:39
  50.3 0.8 copy-start.16
  51.1 0.8 copy-start.20
  51.9 1.0 copy-start.11
  52.9 33.7 %all-to-all-start.2 = ((bf16[8,256,128]{2,1,0:T(8,128)(2,1)}), bf16[8,256,128]{2,1,0:T(8,128)(2,1)S(1)}, u32[]{:S(2)}, u32[]{:S(2)}) async-start(bf16[8,256,128]{2,1,0:T(8,128)(2,1)} %copy-done.20), calls=%async_computation.2 | async-start | bytes 1048576 | tf_op jit(solution)/shard_map/all_to_all | solution.py:354
  70.5 22.1 %copy-start.12 = (bf16[8,512,128]{2,1,0:T(8,128)(2,1)S(1)}, bf16[8,512,128]{2,1,0:T(8,128)(2,1)}, u32[]{:S(2)}) copy-start(bf16[8,512,128]{2,1,0:T(8,128)(2,1)} %copy-done.11) | copy-start | bytes 3145732
  70.6 22.1 %copy-start.25 = (f32[8,128]{1,0:T(8,128)S(1)}, f32[8,128]{1,0:T(8,128)}, u32[]{:S(2)}) copy-start(f32[8,128]{1,0:T(8,128)} %constant.11.clone.sign_ref) | copy-start | bytes 12292
  85.0 0.8 copy-start.18
  85.8 0.9 copy-start.21
  86.6 20.7 %all-to-all-start.1 = ((bf16[8,256,128]{2,1,0:T(8,128)(2,1)}), bf16[8,256,128]{2,1,0:T(8,128)(2,1)}, u32[]{:S(2)}, u32[]{:S(2)}) async-start(bf16[8,256,128]{2,1,0:T(8,128)(2,1)} %copy-done.21), calls=%async_computation.1 | async-start | bytes 1048576 | tf_op jit(solution)/shard_map/all_to_all | solution.py:354
  92.6 1.0 copy-start.14
  95.8 11.5 %copy-start.13 = (bf16[256,1536]{1,0:T(8,128)(2,1)S(1)}, bf16[256,1536]{1,0:T(8,128)(2,1)}, u32[]{:S(2)}) copy-start(bf16[256,1536]{1,0:T(8,128)(2,1)} %constant.12.clone.bwd_ref) | copy-start | bytes 2359300
  99.3 2.0 %copy-start.4 = (f32[2,16,256,128]{3,2,1,0:T(8,128)}, f32[2,16,256,128]{3,2,1,0:T(8,128)S(1)}, u32[]{:S(2)}) copy-start(f32[2,16,256,128]{3,2,1,0:T(8,128)S(1)} %filter_spectra.1.filt_ref) | copy-start | bytes 12582916
  101.3 1.3 copy-start.23
  107.3 2.2 %copy-start.5 = (f32[2,16,256,128]{3,2,1,0:T(8,128)S(1)}, f32[2,16,256,128]{3,2,1,0:T(8,128)}, u32[]{:S(2)}) copy-start(f32[2,16,256,128]{3,2,1,0:T(8,128)} %copy-done.4) | copy-start | bytes 12582916
  109.5 1.0 copy-start.15
  110.5 1.6 copy-start.24
  116.5 1.3 copy-start.7
  117.9 0.8 copy-start.22
  118.7 18.3 %all-to-all-start.3 = ((bf16[8,256,128]{2,1,0:T(8,128)(2,1)}), bf16[8,256,128]{2,1,0:T(8,128)(2,1)S(1)}, u32[]{:S(2)}, u32[]{:S(2)}) async-start(bf16[8,256,128]{2,1,0:T(8,128)(2,1)} %copy-done.22), calls=%async_computation.3 | async-start | bytes 1048576 | tf_op jit(solution)/shard_map/all_to_all | solution.py:354
  122.4 2.2 %copy-start.6 = (f32[2,16,256,128]{3,2,1,0:T(8,128)S(1)}, f32[2,16,256,128]{3,2,1,0:T(8,128)}, u32[]{:S(2)}) copy-start(f32[2,16,256,128]{3,2,1,0:T(8,128)} %copy-done.4) | copy-start | bytes 12582916
  124.6 1.6 copy-start.8
  137.0 3.7 %copy-start.9 = (bf16[8,256,128]{2,1,0:T(8,128)(2,1)}, bf16[8,256,128]{2,1,0:T(8,128)(2,1)S(1)}, u32[]{:S(2)}) copy-start(bf16[8,256,128]{2,1,0:T(8,128)(2,1)S(1)} %all-to-all-done.3.conv_ref) | copy-start | bytes 1572868
  137.0 18.3 %all-to-all-start.4 = ((bf16[8,256,128]{2,1,0:T(8,128)(2,1)}), bf16[8,256,128]{2,1,0:T(8,128)(2,1)S(1)}, u32[]{:S(2)}, u32[]{:S(2)}) async-start(bf16[8,256,128]{2,1,0:T(8,128)(2,1)} %late_blocks.1), calls=%async_computation.4 | async-start | bytes 1048576 | tf_op jit(solution)/shard_map/all_to_all | solution.py:354
  140.7 3.4 %copy-start.2 = (bf16[1024,4096]{1,0:T(8,128)(2,1)S(1)}, bf16[1024,4096]{1,0:T(8,128)(2,1)}, u32[]{:S(2)}) copy-start(bf16[1024,4096]{1,0:T(8,128)(2,1)} %w_ref.3) | copy-start | bytes 25165828
  144.1 1.0 copy-start.10
  145.2 1.0 copy-start.19
  150.7 4.6 %copy-start.17 = (bf16[256,1024]{1,0:T(8,128)(2,1)S(1)}, bf16[256,1024]{1,0:T(8,128)(2,1)}, u32[]{:S(2)}) copy-start(bf16[256,1024]{1,0:T(8,128)(2,1)} %copy-done.16) | copy-start | bytes 1572868
  151.8 12.5 %collective-permute-start.8 = (bf16[256,1024]{1,0:T(8,128)(2,1)}, bf16[256,1024]{1,0:T(8,128)(2,1)}, u32[]{:S(2)}, u32[]{:S(2)}) collective-permute-start(bf16[256,1024]{1,0:T(8,128)(2,1)} %get-tuple-element.22), channel_id=1, source_target_pairs={{0,1},{1,0},{2,3},{3,2},{4,5},{5,4},{6,7},{7,6},{8,9},{9,8},{10,11... | collective-permute-start | bytes 1572872 | tf_op jit(solution)/shard_map/ppermute | solution.py:39
  155.3 3.4 %copy-start.3 = (bf16[1024,4096]{1,0:T(8,128)(2,1)S(1)}, bf16[1024,4096]{1,0:T(8,128)(2,1)}, u32[]{:S(2)}) copy-start(bf16[1024,4096]{1,0:T(8,128)(2,1)} %w_ref.3) | copy-start | bytes 25165828
  163.3 1.0 copy-start.27
  163.3 4.0 %collective-permute-start.11 = (bf16[256,1024]{1,0:T(8,128)(2,1)S(1)}, bf16[256,1024]{1,0:T(8,128)(2,1)S(1)}, u32[]{:S(2)}, u32[]{:S(2)}) collective-permute-start(bf16[256,1024]{1,0:T(8,128)(2,1)S(1)} %get-tuple-element.24), channel_id=1, source_target_pairs={{0,1},{1,0},{2,3},{3,2},{4,5},{5,4},{6,7},{7,6},{8,9},{9,8},{10,11... | collective-permute-start | bytes 1572872 | tf_op jit(solution)/shard_map/ppermute | solution.py:39
  164.3 3.8 %collective-permute-start.7 = (bf16[256,1024]{1,0:T(8,128)(2,1)S(1)}, bf16[256,1024]{1,0:T(8,128)(2,1)S(1)}, u32[]{:S(2)}, u32[]{:S(2)}) collective-permute-start(bf16[256,1024]{1,0:T(8,128)(2,1)S(1)} %copy-done.27), channel_id=1, source_target_pairs={{0,1},{1,0},{2,3},{3,2},{4,5},{5,4},{6,7},{7,6},{8,9},{9,8},{10,11... | collective-permute-start | bytes 1572872 | tf_op jit(solution)/shard_map/ppermute | solution.py:39
  165.5 14.8 %collective-permute-start.9 = (bf16[256,1024]{1,0:T(8,128)(2,1)S(1)}, bf16[256,1024]{1,0:T(8,128)(2,1)S(1)}, u32[]{:S(2)}, u32[]{:S(2)}) collective-permute-start(bf16[256,1024]{1,0:T(8,128)(2,1)S(1)} %fusion.2), channel_id=1, source_target_pairs={{0,2},{1,3},{2,0},{3,1},{4,6},{5,7},{6,4},{7,5},{8,10},{9,11},{10,... | collective-permute-start | bytes 1572872 | tf_op jit(solution)/shard_map/ppermute | solution.py:39
  167.1 13.5 %collective-permute-start.10 = (bf16[256,1024]{1,0:T(8,128)(2,1)S(1)}, bf16[256,1024]{1,0:T(8,128)(2,1)S(1)}, u32[]{:S(2)}, u32[]{:S(2)}) collective-permute-start(bf16[256,1024]{1,0:T(8,128)(2,1)S(1)} %get-tuple-element.23), channel_id=1, source_target_pairs={{0,1},{1,0},{2,3},{3,2},{4,5},{5,4},{6,7},{7,6},{8,9},{9,8},{10,11... | collective-permute-start | bytes 1572872 | tf_op jit(solution)/shard_map/ppermute | solution.py:39
  167.6 23.6 %collective-permute-start.12 = (bf16[256,1024]{1,0:T(8,128)(2,1)S(1)}, bf16[256,1024]{1,0:T(8,128)(2,1)S(1)}, u32[]{:S(2)}, u32[]{:S(2)}) collective-permute-start(bf16[256,1024]{1,0:T(8,128)(2,1)S(1)} %fusion), channel_id=1, source_target_pairs={{0,2},{1,3},{2,0},{3,1},{4,6},{5,7},{6,4},{7,5},{8,10},{9,11},{10,... | collective-permute-start | bytes 1572872 | tf_op jit(solution)/shard_map/ppermute | solution.py:39
  180.3 12.2 %copy-start.1 = (bf16[512,1024]{1,0:T(8,128)(2,1)S(1)}, bf16[512,1024]{1,0:T(8,128)(2,1)}, u32[]{:S(2)}) copy-start(bf16[512,1024]{1,0:T(8,128)(2,1)} %param.11) | copy-start | bytes 3145732
where the time goes:
time: 194 us; the launch traced here: 193 us
  waiting for transfers between devices  56.8 us (29%)
  Pallas kernels  51.3 us (26%)
  starting transfers between devices  48.3 us (25%)
  local copies, waits for them, and re-layouts  32.8 us (17%)
  other arithmetic  3.04 us (2%)
    ppermute x12, waiting for transfers between devices, swap(): return lax.ppermute(shard, axis, [(i, i ^ bit) for i in range(size)])  38.5 us
    all_to_all x5, starting transfers between devices, exchange(): lax.all_to_all(values, 'seq', split_axis=0, concat_axis=0, tiled=True)  38.2 us
    unnamed x58, local copies, waits for them, and re-layouts  30.4 us
    pallas_call x2, Pallas kernels, project(): pl.pallas_call(lambda *refs: project_kernel(count, strip, *refs), grid_sp...  28.8 us
    all_to_all x5, waiting for transfers between devices, exchange(): lax.all_to_all(values, 'seq', split_axis=0, concat_axis=0, tiled=True)  15.6 us
    pallas_call x2, Pallas kernels, output_terms(): pl.pallas_call(output_kernel, grid_spec=pltpu.PrefetchScalarGridSpec(num_...  9.04 us
    ppermute x12, starting transfers between devices, swap(): return lax.ppermute(shard, axis, [(i, i ^ bit) for i in range(size)])  6.21 us
    pallas_call x1, Pallas kernels, middle(): pl.pallas_call(middle_kernel, in_specs=[vmem_spec()] * 5, out_specs=[vmem...  4.39 us
  transfers between devices with their start and end apart: 18, of which 8 were waited for; matrix products, arithmetic and copies ran while one was open for 2% of the time, Pallas kernels for 24%

commit v1 on v0

v1 whole, which is shorter than its diff:
```python
import math

import jax
import jax.numpy as jnp
import numpy as np
from jax import lax
from jax.experimental import pallas as pl
from jax.experimental.pallas import tpu as pltpu
from jax.sharding import PartitionSpec as P

TAPS = 7
HALO = 16
bf16 = jnp.bfloat16
f32 = jnp.float32


def split_parts(table):
    high = table.astype(bf16)
    low = (table - high.astype(np.float64)).astype(bf16)
    return high, low


def fourier_tables(block):
    freqs = np.arange(block)[:, None] + 0.5
    spots = np.arange(block)[None, :]
    angle = 2.0 * math.pi * freqs * spots / (2 * block)
    forward = np.concatenate([np.cos(angle), -np.sin(angle)], 0)
    backward = np.concatenate([np.cos(angle).T, -np.sin(angle).T], 1) / block
    fwd_high, fwd_low = split_parts(forward)
    bwd_high, bwd_low = split_parts(backward)
    fwd = np.concatenate([fwd_high, fwd_low], 1)
    bwd = np.concatenate([bwd_high, bwd_low, bwd_high], 1)
    sign = np.broadcast_to(np.where(np.arange(8) % 2 == 0, 1.0, -1.0)[:, None], (8, 128))
    return fwd, bwd, sign.astype(np.float32)


def swap(shard, axis, bit):
    size = lax.axis_size(axis)
    return lax.ppermute(shard, axis, [(i, i ^ bit) for i in range(size)])


def vmem_spec():
    return pl.BlockSpec(memory_space=pltpu.VMEM)


def hbm_spec():
    return pl.BlockSpec(memory_space=pltpu.HBM)


def pinned(array):
    return pltpu.with_memory_space_constraint(array, pltpu.HBM)


def params(mib):
    return pltpu.CompilerParams(vmem_limit_bytes=mib * 1024 * 1024)


def cost(flops, moved):
    return pl.CostEstimate(flops=flops, bytes_accessed=moved, transcendentals=0)


def project_kernel(pieces, strip, own_ref, *refs):
    x_refs = refs[:pieces]
    w_refs = refs[pieces : 2 * pieces]
    tap_ref, query_ref, product_ref, ext_ref = refs[2 * pieces :]
    rows, width = query_ref.shape
    for branch in range(3):
        total = None
        for x_ref, w_ref in zip(x_refs, w_refs):
            term = jnp.dot(x_ref[...], w_ref[branch], preferred_element_type=f32)
            total = term if total is None else total + term
        ext_ref[branch] = total.astype(bf16).astype(f32)
    step = 64
    for lane in range(0, width, strip):
        lanes = slice(lane, lane + strip)
        for row in range(0, rows, step):

            def mixed(branch):
                running = None
                for offset in range(TAPS):
                    lead = row + HALO - offset
                    term = tap_ref[branch, offset : offset + 1, lanes] * ext_ref[branch, lead : lead + step, lanes]
                    running = term if running is None else running + term
                return running.astype(bf16)

            here = slice(row, row + step)
            query_ref[here, lanes] = mixed(0)
            product = (mixed(1).astype(f32) * mixed(2).astype(f32)).astype(bf16)
            if len(product_ref.shape) == 3:
                product_ref[lane // strip, here, :] = product
            else:
                product_ref[here, lanes] = product


def project(own, pieces, weights, tap_table, blocks):
    count = len(pieces)
    rows_in, depth = pieces[0].shape
    rows = rows_in - HALO
    width = weights.shape[2]
    tile = 256
    chan = width // blocks
    direct = chan % 128 == 0 and tile % chan == 0
    strip = chan if direct else 128
    if direct:
        product_shape = (blocks, rows, chan)
        product_spec = pl.BlockSpec((tile // chan, rows, chan), lambda i, own: (i, 0, 0))
    else:
        product_shape = (rows, width)
        product_spec = pl.BlockSpec((rows, tile), lambda i, own: (0, i))

    def weight_spec(p):
        return pl.BlockSpec((3, depth, tile), lambda i, own: (0, own[0] ^ p, i))

    query, product = pl.pallas_call(
        lambda *refs: project_kernel(count, strip, *refs),
        grid_spec=pltpu.PrefetchScalarGridSpec(
            num_scalar_prefetch=1,
            grid=(width // tile,),
            in_specs=[vmem_spec()] * count
            + [weight_spec(p) for p in range(count)]
            + [pl.BlockSpec((3, TAPS, tile), lambda i, own: (0, 0, i))],
            out_specs=[pl.BlockSpec((rows, tile), lambda i, own: (0, i)), product_spec],
            scratch_shapes=[pltpu.VMEM((3, rows_in, tile), f32)],
        ),
        out_shape=[pltpu.HBM((rows, width), bf16), pltpu.HBM(product_shape, bf16)],
        compiler_params=params(20),
        cost_estimate=cost(2 * rows_in * count * depth * 3 * width, 6 * count * depth * width),
        name="project",
    )(own, *pieces, *([pinned(weights)] * count), tap_table)
    if not direct:
        product = product.reshape(rows, blocks, chan).transpose(1, 0, 2)
    return query, product


def transform_into(fwd_ref, in_ref, picks, out_ref, places):
    block, chan = in_ref.shape[1:]
    group = 2 if chan % 128 == 0 and len(picks) % 2 == 0 else 1
    for start in range(0, len(picks), group):
        signal = jnp.concatenate([in_ref[k] for k in picks[start : start + group]], 1)
        stacked = jnp.concatenate([signal, signal], 0)
        result = jnp.dot(fwd_ref[...], stacked, preferred_element_type=f32)
        for j in range(group):
            lanes = slice(j * chan, (j + 1) * chan)
            out_ref[0, places[start + j]] = result[:block, lanes]
            out_ref[1, places[start + j]] = result[block:, lanes]


def filter_kernel(fwd_ref, sign_ref, taps_ref, out_hbm, out_ref, spec_ref, sem):
    count, block, chan = taps_ref.shape
    transform_into(fwd_ref, taps_ref, range(count), spec_ref, range(count))
    sign = sign_ref[:, :chan]

    def body(i, carry):
        rows = pl.ds(pl.multiple_of(i * 8, 8), 8)
        prev = None
        for k in range(count):
            real, imag = spec_ref[0, k, rows, :], spec_ref[1, k, rows, :]
            if prev is None:
                out_ref[k % 2, 0, k // 2, rows, :] = real
                out_ref[k % 2, 1, k // 2, rows, :] = imag
            else:
                out_ref[k % 2, 0, k // 2, rows, :] = real - sign * prev[1]
                out_ref[k % 2, 1, k // 2, rows, :] = imag + sign * prev[0]
            prev = (real, imag)
        return carry

    lax.fori_loop(0, block // 8, body, 0)
    copy = pltpu.make_async_copy(out_ref, out_hbm, sem)
    copy.start()
    copy.wait()


def filter_spectra(fwd, sign, taps):
    count, block, chan = taps.shape
    shape = (2, 2, count // 2, block, chan)
    return pl.pallas_call(
        filter_kernel,
        in_specs=[vmem_spec()] * 3,
        out_specs=hbm_spec(),
        out_shape=pltpu.HBM(shape, f32),
        scratch_shapes=[
            pltpu.VMEM(shape, f32),
            pltpu.VMEM((2, count, block, chan), f32),
            pltpu.SemaphoreType.DMA,
        ],
        compiler_params=params(16),
        cost_estimate=cost(2 * 2 * count * chan * 4 * block * block, 8 * count * block * chan),
        name="filter_spectra",
    )(fwd, sign, taps)


def accumulate(filt_ref, spec_ref, ahead, init_ref, write):
    half, block, chan = spec_ref.shape[1:]

    def body(i, carry):
        rows = pl.ds(pl.multiple_of(i * 8, 8), 8)
        for target in range(half):
            real = imag = None
            if init_ref is not None:
                real, imag = init_ref[0, target, rows, :], init_ref[1, target, rows, :]
            for source in range(target - ahead + 1):
                lag = target - ahead - source
                xr, xi = spec_ref[0, source, rows, :], spec_ref[1, source, rows, :]
                gr, gi = filt_ref[0, lag, rows, :], filt_ref[1, lag, rows, :]
                if real is None:
                    real, imag = xr * gr - xi * gi, xr * gi + xi * gr
                else:
                    real = real + xr * gr - xi * gi
                    imag = imag + xr * gi + xi * gr
            if real is None:
                real = imag = jnp.zeros((8, chan), f32)
            write(rows, target, real, imag)
        return carry

    lax.fori_loop(0, block // 8, body, 0)


def inverse_block(bwd_ref, sum_ref, out_ref, start):
    chan = sum_ref.shape[2]
    group = inverse_group(sum_ref)
    full = jnp.concatenate([sum_ref[start + j] for j in range(group)], 1)
    high = full.astype(bf16)
    low = (full - high.astype(f32)).astype(bf16)
    stacked = jnp.concatenate([high, high, low], 0)
    result = jnp.dot(bwd_ref[...], stacked, preferred_element_type=f32).astype(out_ref.dtype)
    for j in range(group):
        out_ref[start + j] = result[:, j * chan : (j + 1) * chan]


def inverse_group(sum_ref):
    count, _, chan = sum_ref.shape
    return 2 if chan % 128 == 0 and count % 2 == 0 else 1


def inverse_out(bwd_ref, sum_ref, out_ref, out_hbm, sems):
    count = sum_ref.shape[0]
    group = inverse_group(sum_ref)
    copies = []
    for start in range(0, count, group):
        inverse_block(bwd_ref, sum_ref, out_ref, start)
        here = slice(start, start + group)
        copies.append(pltpu.make_async_copy(out_ref.at[here], out_hbm.at[here], sems.at[start // group]))
        copies[-1].start()
    return copies


def write_sums(sum_ref, block):
    def write(rows, place, real, imag):
        sum_ref[place, rows, :] = real
        sum_ref[place, pl.ds(rows.start + block, 8), :] = imag

    return write


def write_spec(ref):
    def write(rows, place, real, imag):
        ref[0, place, rows, :] = real
        ref[1, place, rows, :] = imag

    return write


def early_kernel(fwd_ref, filt_hbm, half_ref, same_hbm, other_hbm, filt_ref, spec_ref, same_ref, other_ref, sems):
    half = half_ref.shape[0]
    load = pltpu.make_async_copy(filt_hbm, filt_ref, sems.at[0])
    load.start()
    transform_into(fwd_ref, half_ref, range(half), spec_ref, range(half))
    load.wait()
    accumulate(filt_ref.at[0], spec_ref, 0, None, write_spec(same_ref))
    same_out = pltpu.make_async_copy(same_ref, same_hbm, sems.at[1])
    same_out.start()
    accumulate(filt_ref.at[1], spec_ref, 1, None, write_spec(other_ref))
    other_out = pltpu.make_async_copy(other_ref, other_hbm, sems.at[2])
    other_out.start()
    same_out.wait()
    other_out.wait()


def middle_kernel(
    fwd_ref, bwd_ref, filt_hbm, half_ref, init_hbm, out_hbm, spec_hbm,
    filt_ref, init_ref, spec_ref, sum_ref, out_ref, sems, out_sems,
):
    half, block, _ = half_ref.shape
    load_filt = pltpu.make_async_copy(filt_hbm.at[0], filt_ref, sems.at[0])
    load_init = pltpu.make_async_copy(init_hbm, init_ref, sems.at[1])
    load_filt.start()
    load_init.start()
    transform_into(fwd_ref, half_ref, range(half), spec_ref, range(half))
    keep_spec = pltpu.make_async_copy(spec_ref, spec_hbm, sems.at[2])
    keep_spec.start()
    load_filt.wait()
    load_init.wait()
    accumulate(filt_ref, spec_ref, 0, init_ref, write_sums(sum_ref, block))
    copies = inverse_out(bwd_ref, sum_ref, out_ref, out_hbm, out_sems)
    keep_spec.wait()
    for copy in copies:
        copy.wait()


def late_kernel(
    bwd_ref, filt_hbm, spec_hbm, init_hbm, out_hbm,
    filt_ref, spec_ref, init_ref, sum_ref, out_ref, sems, out_sems,
):
    block = spec_ref.shape[2]
    loads = [
        pltpu.make_async_copy(filt_hbm.at[1], filt_ref, sems.at[0]),
        pltpu.make_async_copy(spec_hbm, spec_ref, sems.at[1]),
        pltpu.make_async_copy(init_hbm, init_ref, sems.at[2]),
    ]
    for load in loads:
        load.start()
    for load in loads:
        load.wait()
    accumulate(filt_ref, spec_ref, 0, init_ref, write_sums(sum_ref, block))
    for copy in inverse_out(bwd_ref, sum_ref, out_ref, out_hbm, out_sems):
        copy.wait()


def early(fwd, filt, part):
    half, block, chan = part.shape
    spec = pltpu.HBM((2, half, block, chan), f32)
    return pl.pallas_call(
        early_kernel,
        in_specs=[vmem_spec(), hbm_spec(), vmem_spec()],
        out_specs=[hbm_spec()] * 2,
        out_shape=[spec, spec],
        scratch_shapes=[pltpu.VMEM(filt.shape, f32)]
        + [pltpu.VMEM(spec.shape, f32)] * 3
        + [pltpu.SemaphoreType.DMA((3,))],
        compiler_params=params(32),
        cost_estimate=cost(2 * half * chan * 4 * block * block * 2, 32 * half * block * chan),
        name="early_blocks",
    )(fwd, pinned(filt), part)


def middle(fwd, bwd, filt, part, init):
    half, block, chan = part.shape
    spec = (2, half, block, chan)
    return pl.pallas_call(
        middle_kernel,
        in_specs=[vmem_spec(), vmem_spec(), hbm_spec(), vmem_spec(), hbm_spec()],
        out_specs=[hbm_spec()] * 2,
        out_shape=[pltpu.HBM(part.shape, bf16), pltpu.HBM(spec, f32)],
        scratch_shapes=[pltpu.VMEM(spec, f32)] * 3
        + [pltpu.VMEM((half, 2 * block, chan), f32), pltpu.VMEM(part.shape, bf16)]
        + [pltpu.SemaphoreType.DMA((3,)), pltpu.SemaphoreType.DMA((half,))],
        compiler_params=params(32),
        cost_estimate=cost(2 * half * chan * 10 * block * block * 2, 32 * half * block * chan),
        name="middle_blocks",
    )(fwd, bwd, pinned(filt), part, pinned(init))


def late(bwd, filt, spec, init):
    _, half, block, chan = spec.shape
    return pl.pallas_call(
        late_kernel,
        in_specs=[vmem_spec()] + [hbm_spec()] * 3,
        out_specs=hbm_spec(),
        out_shape=pltpu.HBM((half, block, chan), bf16),
        scratch_shapes=[pltpu.VMEM(spec.shape, f32)] * 3
        + [pltpu.VMEM((half, 2 * block, chan), f32), pltpu.VMEM((half, block, chan), bf16)]
        + [pltpu.SemaphoreType.DMA((3,)), pltpu.SemaphoreType.DMA((half,))],
        compiler_params=params(32),
        cost_estimate=cost(2 * half * chan * 6 * block * block * 2, 32 * half * block * chan),
        name="late_blocks",
    )(bwd, pinned(filt), pinned(spec), pinned(init))


def output_kernel(picks, own_ref, query_ref, conv_ref, w_hbm, *refs):
    count = len(picks)
    out_refs = refs[:count]
    gated_ref, w_ref, sems = refs[count:]
    blocks, _, chan = conv_ref.shape
    wide = out_refs[0].shape[1]
    tile = 512

    def load(slot, col):
        base = (own_ref[0] ^ picks[slot]) * wide + col
        cols = pl.ds(pl.multiple_of(base, tile), tile)
        return pltpu.make_async_copy(w_hbm.at[:, cols], w_ref.at[slot, :, col : col + tile], sems.at[slot, col // tile])

    places = [(slot, col) for slot in range(count) for col in range(0, wide, tile)]
    for place in places:
        load(*place).start()
    for k in range(blocks):
        lanes = slice(k * chan, (k + 1) * chan)
        gated_ref[:, lanes] = (query_ref[:, lanes].astype(f32) * conv_ref[k].astype(f32)).astype(bf16)
    for slot, col in places:
        load(slot, col).wait()
        w = w_ref[slot, :, col : col + tile]
        out_refs[slot][:, col : col + tile] = jnp.dot(gated_ref[...], w, preferred_element_type=f32).astype(bf16)


def output_terms(own, query, conv, weights, parts, picks):
    rows, width = query.shape
    wide = weights.shape[1] // parts
    terms = pl.pallas_call(
        lambda *refs: output_kernel(picks, *refs),
        grid_spec=pltpu.PrefetchScalarGridSpec(
            num_scalar_prefetch=1,
            grid=(),
            in_specs=[vmem_spec()] * 2 + [hbm_spec()],
            out_specs=[vmem_spec()] * len(picks),
            scratch_shapes=[
                pltpu.VMEM((rows, width), bf16),
                pltpu.VMEM((len(picks), width, wide), bf16),
                pltpu.SemaphoreType.DMA((len(picks), wide // 512)),
            ],
        ),
        out_shape=[jax.ShapeDtypeStruct((rows, wide), bf16)] * len(picks),
        compiler_params=params(16),
        cost_estimate=cost(2 * rows * width * len(picks) * wide, 2 * width * len(picks) * wide),
        name="output_terms",
    )(own, query, conv, pinned(weights))
    return dict(zip(picks, terms))


def body(sequence, in_weight, short_weight, filter_taps, out_weight):
    rows, width = sequence.shape
    blocks = lax.axis_size("seq")
    parts = lax.axis_size("ch")
    chan = width // blocks
    block = rows // 2
    fwd, bwd, sign = fourier_tables(block)
    own = lax.axis_index("ch").astype(jnp.int32).reshape(1)
    weights = in_weight.transpose(1, 0, 2)
    tap_table = short_weight.astype(f32).transpose(1, 0, 2)
    bits = [1 << k for k in range(parts.bit_length() - 1)]

    def exchange(values):
        return lax.all_to_all(values, "seq", split_axis=0, concat_axis=0, tiled=True)

    rows_odd = lax.optimization_barrier(sequence[block - HALO :])
    border = lax.ppermute(rows_odd[block:], "seq", [(i, i + 1) for i in range(blocks - 1)])
    filter_taps, border = lax.optimization_barrier((filter_taps, border))
    taps = exchange(filter_taps.reshape(rows, blocks, chan).transpose(1, 0, 2))

    def gather_far(shard):
        pieces = {0: shard}
        for bit in bits[1:]:
            pieces.update({p | bit: swap(piece, "ch", bit) for p, piece in pieces.items()})
        return pieces

    def gather_near(pieces):
        pieces = dict(pieces)
        for bit in bits[:1]:
            pieces.update({p | bit: swap(piece, "ch", bit) for p, piece in pieces.items()})
        return [pieces[p] for p in range(parts)]

    rows_even = jnp.concatenate([border, sequence[:block]], 0)
    far_odd = gather_far(rows_odd)
    rows_even, far_odd = lax.optimization_barrier((rows_even, far_odd))
    far_even = gather_far(rows_even)
    query_odd, product_odd = project(own, gather_near(far_odd), weights, tap_table, blocks)
    product_odd, far_even = lax.optimization_barrier((product_odd, far_even))
    product_odd = exchange(product_odd)
    query_even, product_even = project(own, gather_near(far_even), weights, tap_table, blocks)
    product_even = exchange(product_even)
    filt = filter_spectra(fwd, sign, taps.reshape(2 * blocks, block, chan))
    init_odd, init_even = early(fwd, filt, product_odd)
    conv_even, spec_even = middle(fwd, bwd, filt, product_even, init_even)
    conv_even = exchange(conv_even)
    conv_odd = late(bwd, filt, spec_even, init_odd)
    conv_even, conv_odd = lax.optimization_barrier((conv_even, conv_odd))
    conv_odd = exchange(conv_odd)

    def reduce(held, picked):
        for bit in picked:
            arrived = {p ^ bit: swap(held[p], "ch", bit) for p in held if p & bit}
            held = {p: (held[p].astype(f32) + arrived[p].astype(f32)).astype(bf16) for p in arrived}
        return held

    far, near = list(range(2, parts)), list(range(2))

    def far_sums(query, conv):
        return reduce(output_terms(own, query, conv, out_weight, parts, far), bits[:1])

    def near_sums(query, conv):
        return reduce(output_terms(own, query, conv, out_weight, parts, near), bits[:1])

    far_even = far_sums(query_even, conv_even)
    near_even = near_sums(query_even, conv_even)
    result_even = reduce({**far_even, **near_even}, bits[1:])[0]
    conv_odd, result_even = lax.optimization_barrier((conv_odd, result_even))
    far_odd = far_sums(query_odd, conv_odd)
    near_odd = near_sums(query_odd, conv_odd)
    result_odd = reduce({**far_odd, **near_odd}, bits[1:])[0]
    return jnp.concatenate([result_even, result_odd], 0)


def solution(mesh):
    return jax.shard_map(
        body,
        mesh=mesh,
        in_specs=(
            P("seq", "ch"),
            P(None, None, "ch"),
            P(None, None, "ch"),
            P("seq", "ch"),
            P("ch", None),
        ),
        out_specs=P("seq", "ch"),
        check_vma=False,
    )
```

time: 194 us -> 152 us (0.78)
  local copies, waits for them, and re-layouts: 32.8 us -> 2.4 us
  Pallas kernels: 51.3 us -> 66.4 us
  waiting for transfers between devices: 56.8 us -> 42.9 us
  starting transfers between devices: 48.3 us -> 37.1 us
    unnamed x58 -> x18, local copies, waits for them, and re-layouts: 30.4 us -> 0.05 us
    all_to_all x5, starting transfers between devices: 38.2 us -> 23.5 us  [exchange(): lax.all_to_all(values, 'seq', split_axis=0, concat_axis=0, tiled=True)]
    pallas_call x6 -> x8, Pallas kernels: 22.5 us -> 36.5 us  [the longest x4 12.1 us: output_terms(): pl.pallas_call(lambda *refs: output_kernel(picks, *refs), grid_spec=pltpu...]
    ppermute x12, waiting for transfers between devices: 38.5 us -> 30 us  [swap(): return lax.ppermute(shard, axis, [(i, i ^ bit) for i in range(size)])]
    all_to_all x5, waiting for transfers between devices: 15.6 us -> 12.8 us  [exchange(): lax.all_to_all(values, 'seq', split_axis=0, concat_axis=0, tiled=True)]
    ppermute x1, waiting for transfers between devices: 2.63 us -> 0.01 us  [body(): lax.ppermute(rows_odd[block:], 'seq', [(i, i + 1) for i in range(blocks -...]
    ppermute x12, starting transfers between devices: 6.21 us -> 8.67 us  [swap(): return lax.ppermute(shard, axis, [(i, i ^ bit) for i in range(size)])]
  transfers between devices with their start and end apart: 18 -> 18, of which waited for: 8 -> 7; matrix products, arithmetic and copies ran while one was open for 2% -> 1% of each run, Pallas kernels for 24% -> 35%
where the time goes in v1:
time: 152 us; the launch traced here: 151 us
  Pallas kernels  66.4 us (44%)
  waiting for transfers between devices  42.9 us (28%)
  starting transfers between devices  37.1 us (24%)
  local copies, waits for them, and re-layouts  2.4 us (2%)
  other arithmetic  1.99 us (1%)
    ppermute x12, waiting for transfers between devices, swap(): return lax.ppermute(shard, axis, [(i, i ^ bit) for i in range(size)])  30 us
    pallas_call x2, Pallas kernels, project(): pl.pallas_call(lambda *refs: project_kernel(count, strip, *refs), grid_sp...  29.9 us
    all_to_all x5, starting transfers between devices, exchange(): lax.all_to_all(values, 'seq', split_axis=0, concat_axis=0, tiled=True)  23.5 us
    all_to_all x5, waiting for transfers between devices, exchange(): lax.all_to_all(values, 'seq', split_axis=0, concat_axis=0, tiled=True)  12.8 us
    pallas_call x4, Pallas kernels, output_terms(): pl.pallas_call(lambda *refs: output_kernel(picks, *refs), grid_spec=pltpu...  12.1 us
    ppermute x12, starting transfers between devices, swap(): return lax.ppermute(shard, axis, [(i, i ^ bit) for i in range(size)])  8.67 us
    pallas_call x1, Pallas kernels, middle(): pl.pallas_call(middle_kernel, in_specs=[vmem_spec(), vmem_spec(), hbm_spe...  6.97 us
    pallas_call x1, Pallas kernels, early(): pl.pallas_call(early_kernel, in_specs=[vmem_spec(), hbm_spec(), vmem_spec...  6.9 us
  transfers between devices with their start and end apart: 18, of which 7 were waited for; matrix products, arithmetic and copies ran while one was open for 1% of the time, Pallas kernels for 35%

profile of v1, /device:TPU:0, one launch (start us, length us, event | category | flops | bytes accessed | tf_op | source)
XLA Modules:
  0.0 151.1 jit_solution(3671004139004666263)
XLA Ops:
  0.0 1.2 slice.9.refs_1_
  1.2 0.0 slice-start
  1.2 5.0 %collective-permute-start = (bf16[16,1024]{1,0:T(8,128)(2,1)S(1)}, bf16[16,1024]{1,0:T(8,128)(2,1)S(1)}, u32[]{:S(2)}, u32[]{:S(2)}) collective-permute-start(bf16[16,1024]{1,0:T(8,128)(2,1)S(1)} %slice.12), channel_id=1, source_target_pairs={{0,4},{4,8},{8,12},{12,16},{16,20},{20,24},{24,28},{1,5},{5,9},{9,... | collective-permute-start | bytes 98312 | tf_op jit(solution)/shard_map/ppermute | solution.py:434
  6.2 1.6 %collective-permute-start.1 = (bf16[272,1024]{1,0:T(8,128)(2,1)S(1)}, bf16[272,1024]{1,0:T(8,128)(2,1)S(1)}, u32[]{:S(2)}, u32[]{:S(2)}) collective-permute-start(bf16[272,1024]{1,0:T(8,128)(2,1)S(1)} %slice.9.refs_1_), channel_id=1, source_target_pairs={{0,2},{1,3},{2,0},{3,1},{4,6},{5,7},{6,4},{7,5},{8,10},{9,11},{10,... | collective-permute-start | bytes 1671176 | tf_op jit(solution)/shard_map/ppermute | solution.py:39
  7.8 0.0 collective-permute-done
  7.8 1.2 bitcast_bitcast_fusion
  8.9 6.8 %all-to-all-start = ((bf16[8,512,128]{2,1,0:T(8,128)(2,1)}), bf16[8,512,128]{2,1,0:T(8,128)(2,1)S(1)}, u32[]{:S(2)}, u32[]{:S(2)}) async-start(bf16[8,512,128]{2,1,0:T(8,128)(2,1)} %bitcast_bitcast_fusion), calls=%async_computation | async-start | bytes 2097152 | tf_op jit(solution)/shard_map/all_to_all | solution.py:431
  15.8 4.6 %collective-permute-done.1.refs_3_ = bf16[272,1024]{1,0:T(8,128)(2,1)S(1)} collective-permute-done((bf16[272,1024]{1,0:T(8,128)(2,1)S(1)}, bf16[272,1024]{1,0:T(8,128)(2,1)S(1)}, u32[]{:S(2)}, u32[]{:S(2)}) %collective-permute-start.1) | collective-permute-done | bytes 557088 | tf_op jit(solution)/shard_map/ppermute | solution.py:39
  20.3 0.0 collective-permute-start.2
  20.3 0.5 collective-permute-start.3
  20.9 1.6 %collective-permute-start.4 = (bf16[272,1024]{1,0:T(8,128)(2,1)S(1)}, bf16[272,1024]{1,0:T(8,128)(2,1)}, u32[]{:S(2)}, u32[]{:S(2)}) collective-permute-start(bf16[272,1024]{1,0:T(8,128)(2,1)S(1)} %pad_maximum_fusion.1.refs_1_), channel_id=1, source_target_pairs={{0,2},{1,3},{2,0},{3,1},{4,6},{5,7},{6,4},{7,5},{8,10},{9,11},{10,... | collective-permute-start | bytes 1671176 | tf_op jit(solution)/shard_map/ppermute | solution.py:39
  22.5 0.8 collective-permute-done.3.refs_4_
  23.2 14.9 %project.2 = (bf16[256,1024]{1,0:T(8,128)(2,1)}, bf16[8,256,128]{2,1,0:T(8,128)(2,1)}) custom-call(s32[1]{0:T(128)} %bitcast.2.refs_0_, bf16[272,1024]{1,0:T(8,128)(2,1)S(1)} %slice.9.refs_1_, bf16[272,1024]{1,0:T(8,128)(2,1)} %collective-permute-done.2.refs_2_, bf16[272,1024]{1,0:T(8,128)(2,1)S(1)} %collective-permute-done.1.refs_3_, ...), custom_call_target="tpu_custom_call" | custom-call | flops 6845104128 | bytes 25165824 | tf_op jit(solution)/shard_map/project/pallas_call | solution.py:114
  38.2 0.2 collective-permute-start.5
  38.4 0.4 collective-permute-start.6
  38.7 1.8 %all-to-all-done = bf16[8,512,128]{2,1,0:T(8,128)(2,1)S(1)} async-done(((bf16[8,512,128]{2,1,0:T(8,128)(2,1)}), bf16[8,512,128]{2,1,0:T(8,128)(2,1)S(1)}, u32[]{:S(2)}, u32[]{:S(2)}) %all-to-all-start) | async-done | bytes 1048608 | tf_op jit(solution)/shard_map/all_to_all | solution.py:431
  40.5 3.5 %all-to-all-start.2 = ((bf16[8,256,128]{2,1,0:T(8,128)(2,1)}), bf16[8,256,128]{2,1,0:T(8,128)(2,1)S(1)}, u32[]{:S(2)}, u32[]{:S(2)}) async-start(bf16[8,256,128]{2,1,0:T(8,128)(2,1)} %get-tuple-element.42), calls=%async_computation.2 | async-start | bytes 1048576 | tf_op jit(solution)/shard_map/all_to_all | solution.py:431
  44.0 0.0 copy-start.5
  44.1 0.0 copy-start.7
  44.1 15.0 %project.3 = (bf16[256,1024]{1,0:T(8,128)(2,1)}, bf16[8,256,128]{2,1,0:T(8,128)(2,1)}) custom-call(s32[1]{0:T(128)} %bitcast.2.refs_0_, bf16[272,1024]{1,0:T(8,128)(2,1)S(1)} %pad_maximum_fusion.1.refs_1_, bf16[272,1024]{1,0:T(8,128)(2,1)S(1)} %collective-permute-done.5.refs_2_, bf16[272,1024]{1,0:T(8,128)(2,1)} %collective-permute-done.4.refs_3_, ...), custom_call_target="tpu_custom_call" | custom-call | flops 6845104128 | bytes 25165824 | tf_op jit(solution)/shard_map/project/pallas_call | solution.py:114
  59.1 5.9 %all-to-all-start.1 = ((bf16[8,256,128]{2,1,0:T(8,128)(2,1)}), bf16[8,256,128]{2,1,0:T(8,128)(2,1)S(1)}, u32[]{:S(2)}, u32[]{:S(2)}) async-start(bf16[8,256,128]{2,1,0:T(8,128)(2,1)} %get-tuple-element.41), calls=%async_computation.1 | async-start | bytes 1048576 | tf_op jit(solution)/shard_map/all_to_all | solution.py:431
  65.0 0.0 copy-start.6
  65.0 4.1 %filter_spectra.1.filt_hbm = f32[2,2,8,256,128]{4,3,2,1,0:T(8,128)} custom-call(bf16[512,512]{1,0:T(8,128)(2,1)S(1)} %copy-done.5, f32[8,128]{1,0:T(8,128)S(1)} %copy-done.7, bf16[16,256,128]{2,1,0:T(8,128)(2,1)S(1)} %bitcast.12), custom_call_target="tpu_custom_call" | custom-call | flops 2147483648 | bytes 4194304 | tf_op jit(solution)/shard_map/filter_spectra/pallas_call | solution.py:176
  69.2 0.0 copy-start.4
  69.2 6.9 %early_blocks.1 = (f32[2,8,256,128]{3,2,1,0:T(8,128)}, f32[2,8,256,128]{3,2,1,0:T(8,128)}) custom-call(bf16[512,512]{1,0:T(8,128)(2,1)S(1)} %copy-done.6, f32[2,2,8,256,128]{4,3,2,1,0:T(8,128)} %filter_spectra.1.filt_hbm, bf16[8,256,128]{2,1,0:T(8,128)(2,1)S(1)} %all-to-all-done.2.half_ref), custom_call_target="tpu_custom_call" | custom-call | flops 1073741824 | bytes 8388608 | tf_op jit(solution)/shard_map/early_blocks/pallas_call | solution.py:322
  76.1 3.0 %all-to-all-done.1.half_ref = bf16[8,256,128]{2,1,0:T(8,128)(2,1)S(1)} async-done(((bf16[8,256,128]{2,1,0:T(8,128)(2,1)}), bf16[8,256,128]{2,1,0:T(8,128)(2,1)S(1)}, u32[]{:S(2)}, u32[]{:S(2)}) %all-to-all-start.1) | async-done | bytes 524320 | tf_op jit(solution)/shard_map/all_to_all | solution.py:431
  79.2 7.0 %middle_blocks.1 = (bf16[8,256,128]{2,1,0:T(8,128)(2,1)}, f32[2,8,256,128]{3,2,1,0:T(8,128)}) custom-call(bf16[512,512]{1,0:T(8,128)(2,1)S(1)} %copy-done.6, bf16[256,1536]{1,0:T(8,128)(2,1)S(1)} %copy-done.4, f32[2,2,8,256,128]{4,3,2,1,0:T(8,128)} %filter_spectra.1.filt_hbm, bf16[8,256,128]{2,1,0:T(8,128)(2,1)S(1)} %all-to-all-done.1.half_ref, ...), custom_call_target="tpu_custom_call" | custom-call | flops 2684354560 | bytes 8388608 | tf_op jit(solution)/shard_map/middle_blocks/pallas_call | solution.py:339
  86.1 3.6 %all-to-all-start.3 = ((bf16[8,256,128]{2,1,0:T(8,128)(2,1)}), bf16[8,256,128]{2,1,0:T(8,128)(2,1)S(1)}, u32[]{:S(2)}, u32[]{:S(2)}) async-start(bf16[8,256,128]{2,1,0:T(8,128)(2,1)} %get-tuple-element.44), calls=%async_computation.3 | async-start | bytes 1048576 | tf_op jit(solution)/shard_map/all_to_all | solution.py:431
  89.8 6.4 %late_blocks.1 = bf16[8,256,128]{2,1,0:T(8,128)(2,1)} custom-call(bf16[256,1536]{1,0:T(8,128)(2,1)S(1)} %copy-done.4, f32[2,2,8,256,128]{4,3,2,1,0:T(8,128)} %filter_spectra.1.filt_hbm, f32[2,8,256,128]{3,2,1,0:T(8,128)} %get-tuple-element.45.spec_hbm, f32[2,8,256,128]{3,2,1,0:T(8,128)} %get-tuple-element.46.init_hbm), custom_call_target="tpu_custom_call" | custom-call | flops 1610612736 | bytes 8388608 | tf_op jit(solution)/shard_map/late_blocks/pallas_call | solution.py:355
  96.2 8.0 %all-to-all-done.3.refs_2_ = bf16[8,256,128]{2,1,0:T(8,128)(2,1)S(1)} async-done(((bf16[8,256,128]{2,1,0:T(8,128)(2,1)}), bf16[8,256,128]{2,1,0:T(8,128)(2,1)S(1)}, u32[]{:S(2)}, u32[]{:S(2)}) %all-to-all-start.3) | async-done | bytes 524320 | tf_op jit(solution)/shard_map/all_to_all | solution.py:431
  104.1 3.0 %output_terms.5 = (bf16[256,1024]{1,0:T(8,128)(2,1)S(1)}, bf16[256,1024]{1,0:T(8,128)(2,1)S(1)}) custom-call(s32[1]{0:T(128)} %bitcast.2.refs_0_, bf16[256,1024]{1,0:T(8,128)(2,1)S(1)} %copy-done.3, bf16[8,256,128]{2,1,0:T(8,128)(2,1)S(1)} %all-to-all-done.3.refs_2_, bf16[1024,4096]{1,0:T(8,128)(2,1)} %refs_3_.7), custom_call_target="tpu_custom_call" | custom-call | flops 1073741824 | bytes 4194304 | tf_op jit(solution)/shard_map/output_terms/pallas_call | solution.py:397
  107.2 0.1 collective-permute-start.8
  107.3 3.7 %all-to-all-start.4 = ((bf16[8,256,128]{2,1,0:T(8,128)(2,1)}), bf16[8,256,128]{2,1,0:T(8,128)(2,1)S(1)}, u32[]{:S(2)}, u32[]{:S(2)}) async-start(bf16[8,256,128]{2,1,0:T(8,128)(2,1)} %late_blocks.1), calls=%async_computation.4 | async-start | bytes 1048576 | tf_op jit(solution)/shard_map/all_to_all | solution.py:431
  110.9 3.0 %output_terms.4 = (bf16[256,1024]{1,0:T(8,128)(2,1)S(1)}, bf16[256,1024]{1,0:T(8,128)(2,1)S(1)}) custom-call(s32[1]{0:T(128)} %bitcast.2.refs_0_, bf16[256,1024]{1,0:T(8,128)(2,1)S(1)} %copy-done.3, bf16[8,256,128]{2,1,0:T(8,128)(2,1)S(1)} %all-to-all-done.3.refs_2_, bf16[1024,4096]{1,0:T(8,128)(2,1)} %refs_3_.7), custom_call_target="tpu_custom_call" | custom-call | flops 1073741824 | bytes 4194304 | tf_op jit(solution)/shard_map/output_terms/pallas_call | solution.py:397
  114.0 0.6 collective-permute-start.7
  114.5 0.2 add_convert_fusion.4
  114.7 1.6 %collective-permute-start.9 = (bf16[256,1024]{1,0:T(8,128)(2,1)S(1)}, bf16[256,1024]{1,0:T(8,128)(2,1)S(1)}, u32[]{:S(2)}, u32[]{:S(2)}) collective-permute-start(bf16[256,1024]{1,0:T(8,128)(2,1)S(1)} %add_convert_fusion.4), channel_id=1, source_target_pairs={{0,2},{1,3},{2,0},{3,1},{4,6},{5,7},{6,4},{7,5},{8,10},{9,11},{10,... | collective-permute-start | bytes 1572872 | tf_op jit(solution)/shard_map/ppermute | solution.py:39
  116.3 12.3 %collective-permute-done.9 = bf16[256,1024]{1,0:T(8,128)(2,1)S(1)} collective-permute-done((bf16[256,1024]{1,0:T(8,128)(2,1)S(1)}, bf16[256,1024]{1,0:T(8,128)(2,1)S(1)}, u32[]{:S(2)}, u32[]{:S(2)}) %collective-permute-start.9) | collective-permute-done | bytes 524320 | tf_op jit(solution)/shard_map/ppermute | solution.py:39
  128.7 0.3 add_convert_fusion.3
  129.0 3.0 %output_terms.7 = (bf16[256,1024]{1,0:T(8,128)(2,1)S(1)}, bf16[256,1024]{1,0:T(8,128)(2,1)S(1)}) custom-call(s32[1]{0:T(128)} %bitcast.2.refs_0_, bf16[256,1024]{1,0:T(8,128)(2,1)S(1)} %copy-done.2, bf16[8,256,128]{2,1,0:T(8,128)(2,1)S(1)} %all-to-all-done.4.refs_2_, bf16[1024,4096]{1,0:T(8,128)(2,1)} %refs_3_.7), custom_call_target="tpu_custom_call" | custom-call | flops 1073741824 | bytes 4194304 | tf_op jit(solution)/shard_map/output_terms/pallas_call | solution.py:397
  132.0 0.1 collective-permute-start.11
  132.1 3.0 %output_terms.6 = (bf16[256,1024]{1,0:T(8,128)(2,1)S(1)}, bf16[256,1024]{1,0:T(8,128)(2,1)S(1)}) custom-call(s32[1]{0:T(128)} %bitcast.2.refs_0_, bf16[256,1024]{1,0:T(8,128)(2,1)S(1)} %copy-done.2, bf16[8,256,128]{2,1,0:T(8,128)(2,1)S(1)} %all-to-all-done.4.refs_2_, bf16[1024,4096]{1,0:T(8,128)(2,1)} %refs_3_.7), custom_call_target="tpu_custom_call" | custom-call | flops 1073741824 | bytes 4194304 | tf_op jit(solution)/shard_map/output_terms/pallas_call | solution.py:397
  135.1 0.6 collective-permute-start.10
  135.7 0.2 add_convert_fusion.1
  135.9 1.6 %collective-permute-start.12 = (bf16[256,1024]{1,0:T(8,128)(2,1)S(1)}, bf16[256,1024]{1,0:T(8,128)(2,1)S(1)}, u32[]{:S(2)}, u32[]{:S(2)}) collective-permute-start(bf16[256,1024]{1,0:T(8,128)(2,1)S(1)} %add_convert_fusion.1), channel_id=1, source_target_pairs={{0,2},{1,3},{2,0},{3,1},{4,6},{5,7},{6,4},{7,5},{8,10},{9,11},{10,... | collective-permute-start | bytes 1572872 | tf_op jit(solution)/shard_map/ppermute | solution.py:39
  137.5 12.3 %collective-permute-done.12 = bf16[256,1024]{1,0:T(8,128)(2,1)S(1)} collective-permute-done((bf16[256,1024]{1,0:T(8,128)(2,1)S(1)}, bf16[256,1024]{1,0:T(8,128)(2,1)S(1)}, u32[]{:S(2)}, u32[]{:S(2)}) %collective-permute-start.12) | collective-permute-done | bytes 524320 | tf_op jit(solution)/shard_map/ppermute | solution.py:39
  149.8 0.3 add_convert_fusion
  150.1 1.0 pad_maximum_fusion
  (28 shorter events, 0.1 us)
Async XLA Ops:
  0.0 7.8 %copy-start = (bf16[512,1024]{1,0:T(8,128)(2,1)S(1)}, bf16[512,1024]{1,0:T(8,128)(2,1)}, u32[]{:S(2)}) copy-start(bf16[512,1024]{1,0:T(8,128)(2,1)} %param.11) | copy-start | bytes 3145732
  1.2 14.5 %slice-start = ((bf16[512,1024]{1,0:T(8,128)(2,1)}), bf16[256,1024]{1,0:T(8,128)(2,1)S(1)}, s32[]{:S(2)}) async-start(bf16[512,1024]{1,0:T(8,128)(2,1)} %param.8), calls=%async_computation.5 | async-start | bytes 1048576 | tf_op jit(solution)/shard_map/slice | solution.py:450
  1.2 6.6 %collective-permute-start = (bf16[16,1024]{1,0:T(8,128)(2,1)S(1)}, bf16[16,1024]{1,0:T(8,128)(2,1)S(1)}, u32[]{:S(2)}, u32[]{:S(2)}) collective-permute-start(bf16[16,1024]{1,0:T(8,128)(2,1)S(1)} %slice.12), channel_id=1, source_target_pairs={{0,4},{4,8},{8,12},{12,16},{16,20},{20,24},{24,28},{1,5},{5,9},{9,... | collective-permute-start | bytes 98312 | tf_op jit(solution)/shard_map/ppermute | solution.py:434
  6.2 14.2 %collective-permute-start.1 = (bf16[272,1024]{1,0:T(8,128)(2,1)S(1)}, bf16[272,1024]{1,0:T(8,128)(2,1)S(1)}, u32[]{:S(2)}, u32[]{:S(2)}) collective-permute-start(bf16[272,1024]{1,0:T(8,128)(2,1)S(1)} %slice.9.refs_1_), channel_id=1, source_target_pairs={{0,2},{1,3},{2,0},{3,1},{4,6},{5,7},{6,4},{7,5},{8,10},{9,11},{10,... | collective-permute-start | bytes 1671176 | tf_op jit(solution)/shard_map/ppermute | solution.py:39
  8.9 11.9 %copy-start.8 = (bf16[7,3,1024]{2,0,1:T(8,128)(2,1)S(1)}, bf16[7,3,1024]{2,0,1:T(8,128)(2,1)}, u32[]{:S(2)}) copy-start(bf16[7,3,1024]{2,0,1:T(8,128)(2,1)} %param.10) | copy-start | bytes 129028
  8.9 31.6 %all-to-all-start = ((bf16[8,512,128]{2,1,0:T(8,128)(2,1)}), bf16[8,512,128]{2,1,0:T(8,128)(2,1)S(1)}, u32[]{:S(2)}, u32[]{:S(2)}) async-start(bf16[8,512,128]{2,1,0:T(8,128)(2,1)} %bitcast_bitcast_fusion), calls=%async_computation | async-start | bytes 2097152 | tf_op jit(solution)/shard_map/all_to_all | solution.py:431
  20.3 2.1 %collective-permute-start.2 = (bf16[272,1024]{1,0:T(8,128)(2,1)S(1)}, bf16[272,1024]{1,0:T(8,128)(2,1)}, u32[]{:S(2)}, u32[]{:S(2)}) collective-permute-start(bf16[272,1024]{1,0:T(8,128)(2,1)S(1)} %slice.9.refs_1_), channel_id=1, source_target_pairs={{0,1},{1,0},{2,3},{3,2},{4,5},{5,4},{6,7},{7,6},{8,9},{9,8},{10,11... | collective-permute-start | bytes 1671176 | tf_op jit(solution)/shard_map/ppermute | solution.py:39
  20.3 2.9 %collective-permute-start.3 = (bf16[272,1024]{1,0:T(8,128)(2,1)S(1)}, bf16[272,1024]{1,0:T(8,128)(2,1)}, u32[]{:S(2)}, u32[]{:S(2)}) collective-permute-start(bf16[272,1024]{1,0:T(8,128)(2,1)S(1)} %collective-permute-done.1.refs_3_), channel_id=1, source_target_pairs={{0,1},{1,0},{2,3},{3,2},{4,5},{5,4},{6,7},{7,6},{8,9},{9,8},{10,11... | collective-permute-start | bytes 1671176 | tf_op jit(solution)/shard_map/ppermute | solution.py:39
  20.9 17.3 %collective-permute-start.4 = (bf16[272,1024]{1,0:T(8,128)(2,1)S(1)}, bf16[272,1024]{1,0:T(8,128)(2,1)}, u32[]{:S(2)}, u32[]{:S(2)}) collective-permute-start(bf16[272,1024]{1,0:T(8,128)(2,1)S(1)} %pad_maximum_fusion.1.refs_1_), channel_id=1, source_target_pairs={{0,2},{1,3},{2,0},{3,1},{4,6},{5,7},{6,4},{7,5},{8,10},{9,11},{10,... | collective-permute-start | bytes 1671176 | tf_op jit(solution)/shard_map/ppermute | solution.py:39
  38.2 5.9 %collective-permute-start.5 = (bf16[272,1024]{1,0:T(8,128)(2,1)S(1)}, bf16[272,1024]{1,0:T(8,128)(2,1)S(1)}, u32[]{:S(2)}, u32[]{:S(2)}) collective-permute-start(bf16[272,1024]{1,0:T(8,128)(2,1)S(1)} %pad_maximum_fusion.1.refs_1_), channel_id=1, source_target_pairs={{0,1},{1,0},{2,3},{3,2},{4,5},{5,4},{6,7},{7,6},{8,9},{9,8},{10,11... | collective-permute-start | bytes 1671176 | tf_op jit(solution)/shard_map/ppermute | solution.py:39
  38.4 5.7 %collective-permute-start.6 = (bf16[272,1024]{1,0:T(8,128)(2,1)}, bf16[272,1024]{1,0:T(8,128)(2,1)}, u32[]{:S(2)}, u32[]{:S(2)}) collective-permute-start(bf16[272,1024]{1,0:T(8,128)(2,1)} %collective-permute-done.4.refs_3_), channel_id=1, source_target_pairs={{0,1},{1,0},{2,3},{3,2},{4,5},{5,4},{6,7},{7,6},{8,9},{9,8},{10,11... | collective-permute-start | bytes 1671176 | tf_op jit(solution)/shard_map/ppermute | solution.py:39
  40.5 18.6 %all-to-all-start.2 = ((bf16[8,256,128]{2,1,0:T(8,128)(2,1)}), bf16[8,256,128]{2,1,0:T(8,128)(2,1)S(1)}, u32[]{:S(2)}, u32[]{:S(2)}) async-start(bf16[8,256,128]{2,1,0:T(8,128)(2,1)} %get-tuple-element.42), calls=%async_computation.2 | async-start | bytes 1048576 | tf_op jit(solution)/shard_map/all_to_all | solution.py:431
  44.0 21.0 %copy-start.5 = (bf16[512,512]{1,0:T(8,128)(2,1)S(1)}, bf16[512,512]{1,0:T(8,128)(2,1)}, u32[]{:S(2)}) copy-start(bf16[512,512]{1,0:T(8,128)(2,1)} %constant.10.clone.fwd_ref) | copy-start | bytes 1572868
  44.1 21.0 %copy-start.7 = (f32[8,128]{1,0:T(8,128)S(1)}, f32[8,128]{1,0:T(8,128)}, u32[]{:S(2)}) copy-start(f32[8,128]{1,0:T(8,128)} %constant.11.clone.sign_ref) | copy-start | bytes 12292
  59.1 20.1 %all-to-all-start.1 = ((bf16[8,256,128]{2,1,0:T(8,128)(2,1)}), bf16[8,256,128]{2,1,0:T(8,128)(2,1)S(1)}, u32[]{:S(2)}, u32[]{:S(2)}) async-start(bf16[8,256,128]{2,1,0:T(8,128)(2,1)} %get-tuple-element.41), calls=%async_computation.1 | async-start | bytes 1048576 | tf_op jit(solution)/shard_map/all_to_all | solution.py:431
  65.0 4.2 %copy-start.6 = (bf16[512,512]{1,0:T(8,128)(2,1)S(1)}, bf16[512,512]{1,0:T(8,128)(2,1)}, u32[]{:S(2)}) copy-start(bf16[512,512]{1,0:T(8,128)(2,1)} %constant.10.clone.fwd_ref) | copy-start | bytes 1572868
  69.2 10.0 %copy-start.4 = (bf16[256,1536]{1,0:T(8,128)(2,1)S(1)}, bf16[256,1536]{1,0:T(8,128)(2,1)}, u32[]{:S(2)}) copy-start(bf16[256,1536]{1,0:T(8,128)(2,1)} %constant.12.clone.bwd_ref) | copy-start | bytes 2359300
  86.1 18.0 %all-to-all-start.3 = ((bf16[8,256,128]{2,1,0:T(8,128)(2,1)}), bf16[8,256,128]{2,1,0:T(8,128)(2,1)S(1)}, u32[]{:S(2)}, u32[]{:S(2)}) async-start(bf16[8,256,128]{2,1,0:T(8,128)(2,1)} %get-tuple-element.44), calls=%async_computation.3 | async-start | bytes 1048576 | tf_op jit(solution)/shard_map/all_to_all | solution.py:431
  89.8 14.4 %copy-start.3 = (bf16[256,1024]{1,0:T(8,128)(2,1)S(1)}, bf16[256,1024]{1,0:T(8,128)(2,1)}, u32[]{:S(2)}) copy-start(bf16[256,1024]{1,0:T(8,128)(2,1)} %get-tuple-element.48.refs_1_) | copy-start | bytes 1572868
  107.2 7.4 %collective-permute-start.8 = (bf16[256,1024]{1,0:T(8,128)(2,1)S(1)}, bf16[256,1024]{1,0:T(8,128)(2,1)S(1)}, u32[]{:S(2)}, u32[]{:S(2)}) collective-permute-start(bf16[256,1024]{1,0:T(8,128)(2,1)S(1)} %get-tuple-element.53), channel_id=1, source_target_pairs={{0,1},{1,0},{2,3},{3,2},{4,5},{5,4},{6,7},{7,6},{8,9},{9,8},{10,11... | collective-permute-start | bytes 1572872 | tf_op jit(solution)/shard_map/ppermute | solution.py:39
  107.3 21.7 %all-to-all-start.4 = ((bf16[8,256,128]{2,1,0:T(8,128)(2,1)}), bf16[8,256,128]{2,1,0:T(8,128)(2,1)S(1)}, u32[]{:S(2)}, u32[]{:S(2)}) async-start(bf16[8,256,128]{2,1,0:T(8,128)(2,1)} %late_blocks.1), calls=%async_computation.4 | async-start | bytes 1048576 | tf_op jit(solution)/shard_map/all_to_all | solution.py:431
  114.0 15.0 %copy-start.2 = (bf16[256,1024]{1,0:T(8,128)(2,1)S(1)}, bf16[256,1024]{1,0:T(8,128)(2,1)}, u32[]{:S(2)}) copy-start(bf16[256,1024]{1,0:T(8,128)(2,1)} %get-tuple-element.55.refs_1_) | copy-start | bytes 1572868
  114.0 2.3 %collective-permute-start.7 = (bf16[256,1024]{1,0:T(8,128)(2,1)S(1)}, bf16[256,1024]{1,0:T(8,128)(2,1)S(1)}, u32[]{:S(2)}, u32[]{:S(2)}) collective-permute-start(bf16[256,1024]{1,0:T(8,128)(2,1)S(1)} %get-tuple-element.51), channel_id=1, source_target_pairs={{0,1},{1,0},{2,3},{3,2},{4,5},{5,4},{6,7},{7,6},{8,9},{9,8},{10,11... | collective-permute-start | bytes 1572872 | tf_op jit(solution)/shard_map/ppermute | solution.py:39
  114.7 13.9 %collective-permute-start.9 = (bf16[256,1024]{1,0:T(8,128)(2,1)S(1)}, bf16[256,1024]{1,0:T(8,128)(2,1)S(1)}, u32[]{:S(2)}, u32[]{:S(2)}) collective-permute-start(bf16[256,1024]{1,0:T(8,128)(2,1)S(1)} %add_convert_fusion.4), channel_id=1, source_target_pairs={{0,2},{1,3},{2,0},{3,1},{4,6},{5,7},{6,4},{7,5},{8,10},{9,11},{10,... | collective-permute-start | bytes 1572872 | tf_op jit(solution)/shard_map/ppermute | solution.py:39
  132.0 3.7 %collective-permute-start.11 = (bf16[256,1024]{1,0:T(8,128)(2,1)S(1)}, bf16[256,1024]{1,0:T(8,128)(2,1)S(1)}, u32[]{:S(2)}, u32[]{:S(2)}) collective-permute-start(bf16[256,1024]{1,0:T(8,128)(2,1)S(1)} %get-tuple-element.60), channel_id=1, source_target_pairs={{0,1},{1,0},{2,3},{3,2},{4,5},{5,4},{6,7},{7,6},{8,9},{9,8},{10,11... | collective-permute-start | bytes 1572872 | tf_op jit(solution)/shard_map/ppermute | solution.py:39
  135.1 2.3 %collective-permute-start.10 = (bf16[256,1024]{1,0:T(8,128)(2,1)S(1)}, bf16[256,1024]{1,0:T(8,128)(2,1)S(1)}, u32[]{:S(2)}, u32[]{:S(2)}) collective-permute-start(bf16[256,1024]{1,0:T(8,128)(2,1)S(1)} %get-tuple-element.58), channel_id=1, source_target_pairs={{0,1},{1,0},{2,3},{3,2},{4,5},{5,4},{6,7},{7,6},{8,9},{9,8},{10,11... | collective-permute-start | bytes 1572872 | tf_op jit(solution)/shard_map/ppermute | solution.py:39
  135.9 13.9 %collective-permute-start.12 = (bf16[256,1024]{1,0:T(8,128)(2,1)S(1)}, bf16[256,1024]{1,0:T(8,128)(2,1)S(1)}, u32[]{:S(2)}, u32[]{:S(2)}) collective-permute-start(bf16[256,1024]{1,0:T(8,128)(2,1)S(1)} %add_convert_fusion.1), channel_id=1, source_target_pairs={{0,2},{1,3},{2,0},{3,1},{4,6},{5,7},{6,4},{7,5},{8,10},{9,11},{10,... | collective-permute-start | bytes 1572872 | tf_op jit(solution)/shard_map/ppermute | solution.py:39
  149.8 1.3 copy-start.1

commit v2 on v1

--- a/solution.py
+++ b/solution.py
@@ -10,6 +10,7 @@
 
 TAPS = 7
 HALO = 16
+AHEAD = 3
 bf16 = jnp.bfloat16
 f32 = jnp.float32
 
@@ -189,7 +190,7 @@
     )(fwd, sign, taps)
 
 
-def accumulate(filt_ref, spec_ref, ahead, init_ref, write):
+def accumulate(filt_ref, spec_ref, ahead, init_ref, write, begin=0, end=None):
     half, block, chan = spec_ref.shape[1:]
 
     def body(i, carry):
@@ -212,7 +213,7 @@
             write(rows, target, real, imag)
         return carry
 
-    lax.fori_loop(0, block // 8, body, 0)
+    lax.fori_loop(begin // 8, (block if end is None else end) // 8, body, 0)
 
 
 def inverse_block(bwd_ref, sum_ref, out_ref, start):
@@ -281,16 +282,21 @@
     filt_ref, init_ref, spec_ref, sum_ref, out_ref, sems, out_sems,
 ):
     half, block, _ = half_ref.shape
-    load_filt = pltpu.make_async_copy(filt_hbm.at[0], filt_ref, sems.at[0])
-    load_init = pltpu.make_async_copy(init_hbm, init_ref, sems.at[1])
-    load_filt.start()
-    load_init.start()
+    cut = block // 4
+    loads = []
+    for k in range(4):
+        rows = pl.ds(k * cut, cut)
+        loads.append(pltpu.make_async_copy(filt_hbm.at[0, :, :, rows], filt_ref.at[:, :, rows], sems.at[2 * k]))
+        loads.append(pltpu.make_async_copy(init_hbm.at[:, :, rows], init_ref.at[:, :, rows], sems.at[2 * k + 1]))
+    for load in loads:
+        load.start()
     transform_into(fwd_ref, half_ref, range(half), spec_ref, range(half))
-    keep_spec = pltpu.make_async_copy(spec_ref, spec_hbm, sems.at[2])
+    for k in range(4):
+        loads[2 * k].wait()
+        loads[2 * k + 1].wait()
+        accumulate(filt_ref, spec_ref, 0, init_ref, write_sums(sum_ref, block), k * cut, (k + 1) * cut)
+    keep_spec = pltpu.make_async_copy(spec_ref, spec_hbm, sems.at[8])
     keep_spec.start()
-    load_filt.wait()
-    load_init.wait()
-    accumulate(filt_ref, spec_ref, 0, init_ref, write_sums(sum_ref, block))
     copies = inverse_out(bwd_ref, sum_ref, out_ref, out_hbm, out_sems)
     keep_spec.wait()
     for copy in copies:
@@ -343,7 +349,7 @@
         out_shape=[pltpu.HBM(part.shape, bf16), pltpu.HBM(spec, f32)],
         scratch_shapes=[pltpu.VMEM(spec, f32)] * 3
         + [pltpu.VMEM((half, 2 * block, chan), f32), pltpu.VMEM(part.shape, bf16)]
-        + [pltpu.SemaphoreType.DMA((3,)), pltpu.SemaphoreType.DMA((half,))],
+        + [pltpu.SemaphoreType.DMA((9,)), pltpu.SemaphoreType.DMA((half,))],
         compiler_params=params(32),
         cost_estimate=cost(2 * half * chan * 10 * block * block * 2, 32 * half * block * chan),
         name="middle_blocks",
@@ -380,13 +386,15 @@
         return pltpu.make_async_copy(w_hbm.at[:, cols], w_ref.at[slot, :, col : col + tile], sems.at[slot, col // tile])
 
     places = [(slot, col) for slot in range(count) for col in range(0, wide, tile)]
-    for place in places:
+    for place in places[:AHEAD]:
         load(*place).start()
     for k in range(blocks):
         lanes = slice(k * chan, (k + 1) * chan)
         gated_ref[:, lanes] = (query_ref[:, lanes].astype(f32) * conv_ref[k].astype(f32)).astype(bf16)
-    for slot, col in places:
+    for step, (slot, col) in enumerate(places):
         load(slot, col).wait()
+        for place in places[step + AHEAD :][:1]:
+            load(*place).start()
         w = w_ref[slot, :, col : col + tile]
         out_refs[slot][:, col : col + tile] = jnp.dot(gated_ref[...], w, preferred_element_type=f32).astype(bf16)
 
@@ -408,7 +416,7 @@
             ],
         ),
         out_shape=[jax.ShapeDtypeStruct((rows, wide), bf16)] * len(picks),
-        compiler_params=params(16),
+        compiler_params=params(20),
         cost_estimate=cost(2 * rows * width * len(picks) * wide, 2 * width * len(picks) * wide),
         name="output_terms",
     )(own, query, conv, pinned(weights))
@@ -470,22 +478,13 @@
             held = {p: (held[p].astype(f32) + arrived[p].astype(f32)).astype(bf16) for p in arrived}
         return held
 
-    far, near = list(range(2, parts)), list(range(2))
-
-    def far_sums(query, conv):
-        return reduce(output_terms(own, query, conv, out_weight, parts, far), bits[:1])
-
-    def near_sums(query, conv):
-        return reduce(output_terms(own, query, conv, out_weight, parts, near), bits[:1])
-
-    far_even = far_sums(query_even, conv_even)
-    near_even = near_sums(query_even, conv_even)
-    result_even = reduce({**far_even, **near_even}, bits[1:])[0]
-    conv_odd, result_even = lax.optimization_barrier((conv_odd, result_even))
-    far_odd = far_sums(query_odd, conv_odd)
-    near_odd = near_sums(query_odd, conv_odd)
-    result_odd = reduce({**far_odd, **near_odd}, bits[1:])[0]
-    return jnp.concatenate([result_even, result_odd], 0)
+    everyone = list(range(parts))
+    terms_even = output_terms(own, query_even, conv_even, out_weight, parts, everyone)
+    result_even = reduce(terms_even, bits)[0]
+    terms_odd = output_terms(own, query_odd, conv_odd, out_weight, parts, everyone)
+    sums_odd = reduce(terms_odd, bits[:1])
+    result_even, sums_odd = lax.optimization_barrier((result_even, sums_odd))
+    return jnp.concatenate([result_even, reduce(sums_odd, bits[1:])[0]], 0)
 
 
 def solution(mesh):

time: 152 us -> 144 us (0.947)
  waiting for transfers between devices: 42.9 us -> 38.4 us
  Pallas kernels: 66.4 us -> 62.6 us
    ppermute x12, waiting for transfers between devices: 30 us -> 19.8 us  [swap(): return lax.ppermute(shard, axis, [(i, i ^ bit) for i in range(size)])]
    all_to_all x5, waiting for transfers between devices: 12.8 us -> 18.5 us  [exchange(): lax.all_to_all(values, 'seq', split_axis=0, concat_axis=0, tiled=True)]
    pallas_call x4 -> x2, Pallas kernels: 12.1 us -> 9.95 us  [output_terms(): pl.pallas_call(lambda *refs: output_kernel(picks, *refs), grid_spec=pltpu...]
    pallas_call x1, Pallas kernels: 6.97 us -> 5.24 us  [middle(): pl.pallas_call(middle_kernel, in_specs=[vmem_spec(), vmem_spec(), hbm_spe...]
  transfers between devices with their start and end apart: 18 -> 18, of which waited for: 7 -> 9; matrix products, arithmetic and copies ran while one was open for 1% -> 2% of each run, Pallas kernels for 35% -> 40%
where the time goes in v2:
time: 144 us
  Pallas kernels  62.6 us (43%)
  waiting for transfers between devices  38.4 us (27%)
  starting transfers between devices  37 us (26%)
  other arithmetic  3.15 us (2%)
  local copies, waits for them, and re-layouts  2.4 us (2%)
    pallas_call x2, Pallas kernels, project(): pl.pallas_call(lambda *refs: project_kernel(count, strip, *refs), grid_sp...  29.9 us
    all_to_all x5, starting transfers between devices, exchange(): lax.all_to_all(values, 'seq', split_axis=0, concat_axis=0, tiled=True)  23.5 us
    ppermute x12, waiting for transfers between devices, swap(): return lax.ppermute(shard, axis, [(i, i ^ bit) for i in range(size)])  19.8 us
    all_to_all x5, waiting for transfers between devices, exchange(): lax.all_to_all(values, 'seq', split_axis=0, concat_axis=0, tiled=True)  18.5 us
    pallas_call x2, Pallas kernels, output_terms(): pl.pallas_call(lambda *refs: output_kernel(picks, *refs), grid_spec=pltpu...  9.95 us
    ppermute x12, starting transfers between devices, swap(): return lax.ppermute(shard, axis, [(i, i ^ bit) for i in range(size)])  8.55 us
    pallas_call x1, Pallas kernels, early(): pl.pallas_call(early_kernel, in_specs=[vmem_spec(), hbm_spec(), vmem_spec...  6.9 us
    pallas_call x1, Pallas kernels, late(): pl.pallas_call(late_kernel, in_specs=[vmem_spec()] + [hbm_spec()] * 3, ou...  6.39 us
  transfers between devices with their start and end apart: 18, of which 9 were waited for; matrix products, arithmetic and copies ran while one was open for 2% of the time, Pallas kernels for 40%

profile of v2, /device:TPU:0, one launch (start us, length us, event | category | flops | bytes accessed | tf_op | source)
XLA Modules:
  0.0 143.8 jit_solution(4206897679188897139)
XLA Ops:
  0.0 1.2 slice.9.refs_1_
  1.2 0.0 slice-start
  1.2 5.0 %collective-permute-start = (bf16[16,1024]{1,0:T(8,128)(2,1)S(1)}, bf16[16,1024]{1,0:T(8,128)(2,1)S(1)}, u32[]{:S(2)}, u32[]{:S(2)}) collective-permute-start(bf16[16,1024]{1,0:T(8,128)(2,1)S(1)} %slice.12), channel_id=1, source_target_pairs={{0,4},{4,8},{8,12},{12,16},{16,20},{20,24},{24,28},{1,5},{5,9},{9,... | collective-permute-start | bytes 98312 | tf_op jit(solution)/shard_map/ppermute | solution.py:442
  6.2 1.6 %collective-permute-start.1 = (bf16[272,1024]{1,0:T(8,128)(2,1)S(1)}, bf16[272,1024]{1,0:T(8,128)(2,1)S(1)}, u32[]{:S(2)}, u32[]{:S(2)}) collective-permute-start(bf16[272,1024]{1,0:T(8,128)(2,1)S(1)} %slice.9.refs_1_), channel_id=1, source_target_pairs={{0,2},{1,3},{2,0},{3,1},{4,6},{5,7},{6,4},{7,5},{8,10},{9,11},{10,... | collective-permute-start | bytes 1671176 | tf_op jit(solution)/shard_map/ppermute | solution.py:40
  7.8 1.2 bitcast_bitcast_fusion
  8.9 6.8 %all-to-all-start = ((bf16[8,512,128]{2,1,0:T(8,128)(2,1)}), bf16[8,512,128]{2,1,0:T(8,128)(2,1)S(1)}, u32[]{:S(2)}, u32[]{:S(2)}) async-start(bf16[8,512,128]{2,1,0:T(8,128)(2,1)} %bitcast_bitcast_fusion), calls=%async_computation | async-start | bytes 2097152 | tf_op jit(solution)/shard_map/all_to_all | solution.py:439
  15.8 4.6 %collective-permute-done.1.refs_3_ = bf16[272,1024]{1,0:T(8,128)(2,1)S(1)} collective-permute-done((bf16[272,1024]{1,0:T(8,128)(2,1)S(1)}, bf16[272,1024]{1,0:T(8,128)(2,1)S(1)}, u32[]{:S(2)}, u32[]{:S(2)}) %collective-permute-start.1) | collective-permute-done | bytes 557088 | tf_op jit(solution)/shard_map/ppermute | solution.py:40
  20.3 0.5 collective-permute-start.3
  20.9 1.6 %collective-permute-start.4 = (bf16[272,1024]{1,0:T(8,128)(2,1)S(1)}, bf16[272,1024]{1,0:T(8,128)(2,1)}, u32[]{:S(2)}, u32[]{:S(2)}) collective-permute-start(bf16[272,1024]{1,0:T(8,128)(2,1)S(1)} %pad_maximum_fusion.1.refs_1_), channel_id=1, source_target_pairs={{0,2},{1,3},{2,0},{3,1},{4,6},{5,7},{6,4},{7,5},{8,10},{9,11},{10,... | collective-permute-start | bytes 1671176 | tf_op jit(solution)/shard_map/ppermute | solution.py:40
  22.5 0.8 collective-permute-done.3.refs_4_
  23.2 14.9 %project.2 = (bf16[256,1024]{1,0:T(8,128)(2,1)}, bf16[8,256,128]{2,1,0:T(8,128)(2,1)}) custom-call(s32[1]{0:T(128)} %bitcast.refs_0_, bf16[272,1024]{1,0:T(8,128)(2,1)S(1)} %slice.9.refs_1_, bf16[272,1024]{1,0:T(8,128)(2,1)} %collective-permute-done.2.refs_2_, bf16[272,1024]{1,0:T(8,128)(2,1)S(1)} %collective-permute-done.1.refs_3_, ...), custom_call_target="tpu_custom_call" | custom-call | flops 6845104128 | bytes 25165824 | tf_op jit(solution)/shard_map/project/pallas_call | solution.py:115
  38.2 0.2 collective-permute-start.5
  38.4 0.4 collective-permute-start.6
  38.7 1.8 %all-to-all-done = bf16[8,512,128]{2,1,0:T(8,128)(2,1)S(1)} async-done(((bf16[8,512,128]{2,1,0:T(8,128)(2,1)}), bf16[8,512,128]{2,1,0:T(8,128)(2,1)S(1)}, u32[]{:S(2)}, u32[]{:S(2)}) %all-to-all-start) | async-done | bytes 1048608 | tf_op jit(solution)/shard_map/all_to_all | solution.py:439
  40.5 3.5 %all-to-all-start.2 = ((bf16[8,256,128]{2,1,0:T(8,128)(2,1)}), bf16[8,256,128]{2,1,0:T(8,128)(2,1)S(1)}, u32[]{:S(2)}, u32[]{:S(2)}) async-start(bf16[8,256,128]{2,1,0:T(8,128)(2,1)} %get-tuple-element.44), calls=%async_computation.2 | async-start | bytes 1048576 | tf_op jit(solution)/shard_map/all_to_all | solution.py:439
  44.0 0.0 copy-start.4
  44.1 0.0 copy-start.7
  44.1 15.0 %project.3 = (bf16[256,1024]{1,0:T(8,128)(2,1)}, bf16[8,256,128]{2,1,0:T(8,128)(2,1)}) custom-call(s32[1]{0:T(128)} %bitcast.refs_0_, bf16[272,1024]{1,0:T(8,128)(2,1)S(1)} %pad_maximum_fusion.1.refs_1_, bf16[272,1024]{1,0:T(8,128)(2,1)S(1)} %collective-permute-done.5.refs_2_, bf16[272,1024]{1,0:T(8,128)(2,1)} %collective-permute-done.4.refs_3_, ...), custom_call_target="tpu_custom_call" | custom-call | flops 6845104128 | bytes 25165824 | tf_op jit(solution)/shard_map/project/pallas_call | solution.py:115
  59.1 5.9 %all-to-all-start.1 = ((bf16[8,256,128]{2,1,0:T(8,128)(2,1)}), bf16[8,256,128]{2,1,0:T(8,128)(2,1)S(1)}, u32[]{:S(2)}, u32[]{:S(2)}) async-start(bf16[8,256,128]{2,1,0:T(8,128)(2,1)} %get-tuple-element.43), calls=%async_computation.1 | async-start | bytes 1048576 | tf_op jit(solution)/shard_map/all_to_all | solution.py:439
  65.0 0.0 copy-start.5
  65.0 4.1 %filter_spectra.1.filt_hbm = f32[2,2,8,256,128]{4,3,2,1,0:T(8,128)} custom-call(bf16[512,512]{1,0:T(8,128)(2,1)S(1)} %copy-done.4, f32[8,128]{1,0:T(8,128)S(1)} %copy-done.7, bf16[16,256,128]{2,1,0:T(8,128)(2,1)S(1)} %bitcast.12), custom_call_target="tpu_custom_call" | custom-call | flops 2147483648 | bytes 4194304 | tf_op jit(solution)/shard_map/filter_spectra/pallas_call | solution.py:177
  69.2 0.0 copy-start.2
  69.2 6.9 %early_blocks.1 = (f32[2,8,256,128]{3,2,1,0:T(8,128)}, f32[2,8,256,128]{3,2,1,0:T(8,128)}) custom-call(bf16[512,512]{1,0:T(8,128)(2,1)S(1)} %copy-done.5, f32[2,2,8,256,128]{4,3,2,1,0:T(8,128)} %filter_spectra.1.filt_hbm, bf16[8,256,128]{2,1,0:T(8,128)(2,1)S(1)} %all-to-all-done.2.half_ref), custom_call_target="tpu_custom_call" | custom-call | flops 1073741824 | bytes 8388608 | tf_op jit(solution)/shard_map/early_blocks/pallas_call | solution.py:328
  76.1 3.0 %all-to-all-done.1.half_ref = bf16[8,256,128]{2,1,0:T(8,128)(2,1)S(1)} async-done(((bf16[8,256,128]{2,1,0:T(8,128)(2,1)}), bf16[8,256,128]{2,1,0:T(8,128)(2,1)S(1)}, u32[]{:S(2)}, u32[]{:S(2)}) %all-to-all-start.1) | async-done | bytes 524320 | tf_op jit(solution)/shard_map/all_to_all | solution.py:439
  79.2 5.2 %middle_blocks.1 = (bf16[8,256,128]{2,1,0:T(8,128)(2,1)}, f32[2,8,256,128]{3,2,1,0:T(8,128)}) custom-call(bf16[512,512]{1,0:T(8,128)(2,1)S(1)} %copy-done.5, bf16[256,1536]{1,0:T(8,128)(2,1)S(1)} %copy-done.2, f32[2,2,8,256,128]{4,3,2,1,0:T(8,128)} %filter_spectra.1.filt_hbm, bf16[8,256,128]{2,1,0:T(8,128)(2,1)S(1)} %all-to-all-done.1.half_ref, ...), custom_call_target="tpu_custom_call" | custom-call | flops 2684354560 | bytes 8388608 | tf_op jit(solution)/shard_map/middle_blocks/pallas_call | solution.py:345
  84.4 3.6 %all-to-all-start.3 = ((bf16[8,256,128]{2,1,0:T(8,128)(2,1)}), bf16[8,256,128]{2,1,0:T(8,128)(2,1)S(1)}, u32[]{:S(2)}, u32[]{:S(2)}) async-start(bf16[8,256,128]{2,1,0:T(8,128)(2,1)} %get-tuple-element.46), calls=%async_computation.3 | async-start | bytes 1048576 | tf_op jit(solution)/shard_map/all_to_all | solution.py:439
  88.0 6.4 %late_blocks.1 = bf16[8,256,128]{2,1,0:T(8,128)(2,1)} custom-call(bf16[256,1536]{1,0:T(8,128)(2,1)S(1)} %copy-done.2, f32[2,2,8,256,128]{4,3,2,1,0:T(8,128)} %filter_spectra.1.filt_hbm, f32[2,8,256,128]{3,2,1,0:T(8,128)} %get-tuple-element.47.spec_hbm, f32[2,8,256,128]{3,2,1,0:T(8,128)} %get-tuple-element.48.init_hbm), custom_call_target="tpu_custom_call" | custom-call | flops 1610612736 | bytes 8388608 | tf_op jit(solution)/shard_map/late_blocks/pallas_call | solution.py:361
  94.4 7.9 %all-to-all-done.3.refs_2_ = bf16[8,256,128]{2,1,0:T(8,128)(2,1)S(1)} async-done(((bf16[8,256,128]{2,1,0:T(8,128)(2,1)}), bf16[8,256,128]{2,1,0:T(8,128)(2,1)S(1)}, u32[]{:S(2)}, u32[]{:S(2)}) %all-to-all-start.3) | async-done | bytes 524320 | tf_op jit(solution)/shard_map/all_to_all | solution.py:439
  102.4 3.7 %all-to-all-start.4 = ((bf16[8,256,128]{2,1,0:T(8,128)(2,1)}), bf16[8,256,128]{2,1,0:T(8,128)(2,1)S(1)}, u32[]{:S(2)}, u32[]{:S(2)}) async-start(bf16[8,256,128]{2,1,0:T(8,128)(2,1)} %late_blocks.1), calls=%async_computation.4 | async-start | bytes 1048576 | tf_op jit(solution)/shard_map/all_to_all | solution.py:439
  106.1 5.0 %output_terms.2 = (bf16[256,1024]{1,0:T(8,128)(2,1)S(1)}, bf16[256,1024]{1,0:T(8,128)(2,1)S(1)}, bf16[256,1024]{1,0:T(8,128)(2,1)S(1)}, bf16[256,1024]{1,0:T(8,128)(2,1)S(1)}) custom-call(s32[1]{0:T(128)} %bitcast.refs_0_, bf16[256,1024]{1,0:T(8,128)(2,1)S(1)} %copy-done.6, bf16[8,256,128]{2,1,0:T(8,128)(2,1)S(1)} %all-to-all-done.3.refs_2_, ...), custom_call_target="tpu_custom_call" | custom-call | flops 2147483648 | bytes 8388608 | tf_op jit(solution)/shard_map/output_terms/pallas_call | solution.py:405
  111.1 0.1 collective-permute-start.8
  111.2 0.5 collective-permute-start.7
  111.7 1.4 collective-permute-done.8
  113.1 0.2 add_convert_fusion.4
  113.3 1.6 %collective-permute-start.9 = (bf16[256,1024]{1,0:T(8,128)(2,1)S(1)}, bf16[256,1024]{1,0:T(8,128)(2,1)}, u32[]{:S(2)}, u32[]{:S(2)}) collective-permute-start(bf16[256,1024]{1,0:T(8,128)(2,1)S(1)} %add_convert_fusion.4), channel_id=1, source_target_pairs={{0,2},{1,3},{2,0},{3,1},{4,6},{5,7},{6,4},{7,5},{8,10},{9,11},{10,... | collective-permute-start | bytes 1572872 | tf_op jit(solution)/shard_map/ppermute | solution.py:40
  114.9 5.8 %all-to-all-done.4.refs_2_ = bf16[8,256,128]{2,1,0:T(8,128)(2,1)S(1)} async-done(((bf16[8,256,128]{2,1,0:T(8,128)(2,1)}), bf16[8,256,128]{2,1,0:T(8,128)(2,1)S(1)}, u32[]{:S(2)}, u32[]{:S(2)}) %all-to-all-start.4) | async-done | bytes 524320 | tf_op jit(solution)/shard_map/all_to_all | solution.py:439
  120.6 4.9 %output_terms.3 = (bf16[256,1024]{1,0:T(8,128)(2,1)S(1)}, bf16[256,1024]{1,0:T(8,128)(2,1)S(1)}, bf16[256,1024]{1,0:T(8,128)(2,1)S(1)}, bf16[256,1024]{1,0:T(8,128)(2,1)S(1)}) custom-call(s32[1]{0:T(128)} %bitcast.refs_0_, bf16[256,1024]{1,0:T(8,128)(2,1)S(1)} %copy-done.3, bf16[8,256,128]{2,1,0:T(8,128)(2,1)S(1)} %all-to-all-done.4.refs_2_, ...), custom_call_target="tpu_custom_call" | custom-call | flops 2147483648 | bytes 8388608 | tf_op jit(solution)/shard_map/output_terms/pallas_call | solution.py:405
  125.6 0.1 collective-permute-start.10
  125.7 0.5 collective-permute-start.11
  126.2 1.3 collective-permute-done.9
  127.4 1.3 add_convert_fusion.3
  128.7 0.2 add_convert_fusion.2
  128.9 0.0 copy-start.1
  129.0 0.2 add_convert_fusion.1
  129.2 1.6 %collective-permute-start.12 = (bf16[256,1024]{1,0:T(8,128)(2,1)S(1)}, bf16[256,1024]{1,0:T(8,128)(2,1)S(1)}, u32[]{:S(2)}, u32[]{:S(2)}) collective-permute-start(bf16[256,1024]{1,0:T(8,128)(2,1)S(1)} %add_convert_fusion.1), channel_id=1, source_target_pairs={{0,2},{1,3},{2,0},{3,1},{4,6},{5,7},{6,4},{7,5},{8,10},{9,11},{10,... | collective-permute-start | bytes 1572872 | tf_op jit(solution)/shard_map/ppermute | solution.py:40
  130.7 11.8 %collective-permute-done.12 = bf16[256,1024]{1,0:T(8,128)(2,1)S(1)} collective-permute-done((bf16[256,1024]{1,0:T(8,128)(2,1)S(1)}, bf16[256,1024]{1,0:T(8,128)(2,1)S(1)}, u32[]{:S(2)}, u32[]{:S(2)}) %collective-permute-start.12) | collective-permute-done | bytes 524320 | tf_op jit(solution)/shard_map/ppermute | solution.py:40
  142.5 0.2 add_convert_fusion
  142.7 1.0 pad_maximum_fusion
  (27 shorter events, 0.1 us)
Async XLA Ops:
  0.0 7.8 %copy-start = (bf16[512,1024]{1,0:T(8,128)(2,1)S(1)}, bf16[512,1024]{1,0:T(8,128)(2,1)}, u32[]{:S(2)}) copy-start(bf16[512,1024]{1,0:T(8,128)(2,1)} %param.11) | copy-start | bytes 3145732
  1.2 14.5 %slice-start = ((bf16[512,1024]{1,0:T(8,128)(2,1)}), bf16[256,1024]{1,0:T(8,128)(2,1)S(1)}, s32[]{:S(2)}) async-start(bf16[512,1024]{1,0:T(8,128)(2,1)} %param.8), calls=%async_computation.5 | async-start | bytes 1048576 | tf_op jit(solution)/shard_map/slice | solution.py:458
  1.2 6.6 %collective-permute-start = (bf16[16,1024]{1,0:T(8,128)(2,1)S(1)}, bf16[16,1024]{1,0:T(8,128)(2,1)S(1)}, u32[]{:S(2)}, u32[]{:S(2)}) collective-permute-start(bf16[16,1024]{1,0:T(8,128)(2,1)S(1)} %slice.12), channel_id=1, source_target_pairs={{0,4},{4,8},{8,12},{12,16},{16,20},{20,24},{24,28},{1,5},{5,9},{9,... | collective-permute-start | bytes 98312 | tf_op jit(solution)/shard_map/ppermute | solution.py:442
  6.2 14.2 %collective-permute-start.1 = (bf16[272,1024]{1,0:T(8,128)(2,1)S(1)}, bf16[272,1024]{1,0:T(8,128)(2,1)S(1)}, u32[]{:S(2)}, u32[]{:S(2)}) collective-permute-start(bf16[272,1024]{1,0:T(8,128)(2,1)S(1)} %slice.9.refs_1_), channel_id=1, source_target_pairs={{0,2},{1,3},{2,0},{3,1},{4,6},{5,7},{6,4},{7,5},{8,10},{9,11},{10,... | collective-permute-start | bytes 1671176 | tf_op jit(solution)/shard_map/ppermute | solution.py:40
  8.9 11.9 %copy-start.8 = (bf16[7,3,1024]{2,0,1:T(8,128)(2,1)S(1)}, bf16[7,3,1024]{2,0,1:T(8,128)(2,1)}, u32[]{:S(2)}) copy-start(bf16[7,3,1024]{2,0,1:T(8,128)(2,1)} %param.10) | copy-start | bytes 129028
  8.9 31.6 %all-to-all-start = ((bf16[8,512,128]{2,1,0:T(8,128)(2,1)}), bf16[8,512,128]{2,1,0:T(8,128)(2,1)S(1)}, u32[]{:S(2)}, u32[]{:S(2)}) async-start(bf16[8,512,128]{2,1,0:T(8,128)(2,1)} %bitcast_bitcast_fusion), calls=%async_computation | async-start | bytes 2097152 | tf_op jit(solution)/shard_map/all_to_all | solution.py:439
  20.3 2.1 %collective-permute-start.2 = (bf16[272,1024]{1,0:T(8,128)(2,1)S(1)}, bf16[272,1024]{1,0:T(8,128)(2,1)}, u32[]{:S(2)}, u32[]{:S(2)}) collective-permute-start(bf16[272,1024]{1,0:T(8,128)(2,1)S(1)} %slice.9.refs_1_), channel_id=1, source_target_pairs={{0,1},{1,0},{2,3},{3,2},{4,5},{5,4},{6,7},{7,6},{8,9},{9,8},{10,11... | collective-permute-start | bytes 1671176 | tf_op jit(solution)/shard_map/ppermute | solution.py:40
  20.3 2.9 %collective-permute-start.3 = (bf16[272,1024]{1,0:T(8,128)(2,1)S(1)}, bf16[272,1024]{1,0:T(8,128)(2,1)}, u32[]{:S(2)}, u32[]{:S(2)}) collective-permute-start(bf16[272,1024]{1,0:T(8,128)(2,1)S(1)} %collective-permute-done.1.refs_3_), channel_id=1, source_target_pairs={{0,1},{1,0},{2,3},{3,2},{4,5},{5,4},{6,7},{7,6},{8,9},{9,8},{10,11... | collective-permute-start | bytes 1671176 | tf_op jit(solution)/shard_map/ppermute | solution.py:40
  20.9 17.3 %collective-permute-start.4 = (bf16[272,1024]{1,0:T(8,128)(2,1)S(1)}, bf16[272,1024]{1,0:T(8,128)(2,1)}, u32[]{:S(2)}, u32[]{:S(2)}) collective-permute-start(bf16[272,1024]{1,0:T(8,128)(2,1)S(1)} %pad_maximum_fusion.1.refs_1_), channel_id=1, source_target_pairs={{0,2},{1,3},{2,0},{3,1},{4,6},{5,7},{6,4},{7,5},{8,10},{9,11},{10,... | collective-permute-start | bytes 1671176 | tf_op jit(solution)/shard_map/ppermute | solution.py:40
  38.2 5.9 %collective-permute-start.5 = (bf16[272,1024]{1,0:T(8,128)(2,1)S(1)}, bf16[272,1024]{1,0:T(8,128)(2,1)S(1)}, u32[]{:S(2)}, u32[]{:S(2)}) collective-permute-start(bf16[272,1024]{1,0:T(8,128)(2,1)S(1)} %pad_maximum_fusion.1.refs_1_), channel_id=1, source_target_pairs={{0,1},{1,0},{2,3},{3,2},{4,5},{5,4},{6,7},{7,6},{8,9},{9,8},{10,11... | collective-permute-start | bytes 1671176 | tf_op jit(solution)/shard_map/ppermute | solution.py:40
  38.4 5.7 %collective-permute-start.6 = (bf16[272,1024]{1,0:T(8,128)(2,1)}, bf16[272,1024]{1,0:T(8,128)(2,1)}, u32[]{:S(2)}, u32[]{:S(2)}) collective-permute-start(bf16[272,1024]{1,0:T(8,128)(2,1)} %collective-permute-done.4.refs_3_), channel_id=1, source_target_pairs={{0,1},{1,0},{2,3},{3,2},{4,5},{5,4},{6,7},{7,6},{8,9},{9,8},{10,11... | collective-permute-start | bytes 1671176 | tf_op jit(solution)/shard_map/ppermute | solution.py:40
  40.5 18.5 %all-to-all-start.2 = ((bf16[8,256,128]{2,1,0:T(8,128)(2,1)}), bf16[8,256,128]{2,1,0:T(8,128)(2,1)S(1)}, u32[]{:S(2)}, u32[]{:S(2)}) async-start(bf16[8,256,128]{2,1,0:T(8,128)(2,1)} %get-tuple-element.44), calls=%async_computation.2 | async-start | bytes 1048576 | tf_op jit(solution)/shard_map/all_to_all | solution.py:439
  44.0 21.0 %copy-start.4 = (bf16[512,512]{1,0:T(8,128)(2,1)S(1)}, bf16[512,512]{1,0:T(8,128)(2,1)}, u32[]{:S(2)}) copy-start(bf16[512,512]{1,0:T(8,128)(2,1)} %constant.10.clone.fwd_ref) | copy-start | bytes 1572868
  44.1 21.0 %copy-start.7 = (f32[8,128]{1,0:T(8,128)S(1)}, f32[8,128]{1,0:T(8,128)}, u32[]{:S(2)}) copy-start(f32[8,128]{1,0:T(8,128)} %constant.11.clone.sign_ref) | copy-start | bytes 12292
  59.1 20.1 %all-to-all-start.1 = ((bf16[8,256,128]{2,1,0:T(8,128)(2,1)}), bf16[8,256,128]{2,1,0:T(8,128)(2,1)S(1)}, u32[]{:S(2)}, u32[]{:S(2)}) async-start(bf16[8,256,128]{2,1,0:T(8,128)(2,1)} %get-tuple-element.43), calls=%async_computation.1 | async-start | bytes 1048576 | tf_op jit(solution)/shard_map/all_to_all | solution.py:439
  65.0 4.2 %copy-start.5 = (bf16[512,512]{1,0:T(8,128)(2,1)S(1)}, bf16[512,512]{1,0:T(8,128)(2,1)}, u32[]{:S(2)}) copy-start(bf16[512,512]{1,0:T(8,128)(2,1)} %constant.10.clone.fwd_ref) | copy-start | bytes 1572868
  69.2 10.0 %copy-start.2 = (bf16[256,1536]{1,0:T(8,128)(2,1)S(1)}, bf16[256,1536]{1,0:T(8,128)(2,1)}, u32[]{:S(2)}) copy-start(bf16[256,1536]{1,0:T(8,128)(2,1)} %constant.12.clone.bwd_ref) | copy-start | bytes 2359300
  84.4 18.0 %all-to-all-start.3 = ((bf16[8,256,128]{2,1,0:T(8,128)(2,1)}), bf16[8,256,128]{2,1,0:T(8,128)(2,1)S(1)}, u32[]{:S(2)}, u32[]{:S(2)}) async-start(bf16[8,256,128]{2,1,0:T(8,128)(2,1)} %get-tuple-element.46), calls=%async_computation.3 | async-start | bytes 1048576 | tf_op jit(solution)/shard_map/all_to_all | solution.py:439
  88.0 18.0 %copy-start.6 = (bf16[256,1024]{1,0:T(8,128)(2,1)S(1)}, bf16[256,1024]{1,0:T(8,128)(2,1)}, u32[]{:S(2)}) copy-start(bf16[256,1024]{1,0:T(8,128)(2,1)} %get-tuple-element.41.refs_1_) | copy-start | bytes 1572868
  102.4 18.2 %all-to-all-start.4 = ((bf16[8,256,128]{2,1,0:T(8,128)(2,1)}), bf16[8,256,128]{2,1,0:T(8,128)(2,1)S(1)}, u32[]{:S(2)}, u32[]{:S(2)}) async-start(bf16[8,256,128]{2,1,0:T(8,128)(2,1)} %late_blocks.1), calls=%async_computation.4 | async-start | bytes 1048576 | tf_op jit(solution)/shard_map/all_to_all | solution.py:439
  106.1 14.5 %copy-start.3 = (bf16[256,1024]{1,0:T(8,128)(2,1)S(1)}, bf16[256,1024]{1,0:T(8,128)(2,1)}, u32[]{:S(2)}) copy-start(bf16[256,1024]{1,0:T(8,128)(2,1)} %get-tuple-element.54.refs_1_) | copy-start | bytes 1572868
  111.1 2.0 %collective-permute-start.8 = (bf16[256,1024]{1,0:T(8,128)(2,1)S(1)}, bf16[256,1024]{1,0:T(8,128)(2,1)S(1)}, u32[]{:S(2)}, u32[]{:S(2)}) collective-permute-start(bf16[256,1024]{1,0:T(8,128)(2,1)S(1)} %get-tuple-element.53), channel_id=1, source_target_pairs={{0,1},{1,0},{2,3},{3,2},{4,5},{5,4},{6,7},{7,6},{8,9},{9,8},{10,11... | collective-permute-start | bytes 1572872 | tf_op jit(solution)/shard_map/ppermute | solution.py:40
  111.2 15.0 %collective-permute-start.7 = (bf16[256,1024]{1,0:T(8,128)(2,1)S(1)}, bf16[256,1024]{1,0:T(8,128)(2,1)S(1)}, u32[]{:S(2)}, u32[]{:S(2)}) collective-permute-start(bf16[256,1024]{1,0:T(8,128)(2,1)S(1)} %get-tuple-element.51), channel_id=1, source_target_pairs={{0,1},{1,0},{2,3},{3,2},{4,5},{5,4},{6,7},{7,6},{8,9},{9,8},{10,11... | collective-permute-start | bytes 1572872 | tf_op jit(solution)/shard_map/ppermute | solution.py:40
  113.3 14.1 %collective-permute-start.9 = (bf16[256,1024]{1,0:T(8,128)(2,1)S(1)}, bf16[256,1024]{1,0:T(8,128)(2,1)}, u32[]{:S(2)}, u32[]{:S(2)}) collective-permute-start(bf16[256,1024]{1,0:T(8,128)(2,1)S(1)} %add_convert_fusion.4), channel_id=1, source_target_pairs={{0,2},{1,3},{2,0},{3,1},{4,6},{5,7},{6,4},{7,5},{8,10},{9,11},{10,... | collective-permute-start | bytes 1572872 | tf_op jit(solution)/shard_map/ppermute | solution.py:40
  125.6 3.2 %collective-permute-start.10 = (bf16[256,1024]{1,0:T(8,128)(2,1)S(1)}, bf16[256,1024]{1,0:T(8,128)(2,1)S(1)}, u32[]{:S(2)}, u32[]{:S(2)}) collective-permute-start(bf16[256,1024]{1,0:T(8,128)(2,1)S(1)} %get-tuple-element.57), channel_id=1, source_target_pairs={{0,1},{1,0},{2,3},{3,2},{4,5},{5,4},{6,7},{7,6},{8,9},{9,8},{10,11... | collective-permute-start | bytes 1572872 | tf_op jit(solution)/shard_map/ppermute | solution.py:40
  125.7 3.3 %collective-permute-start.11 = (bf16[256,1024]{1,0:T(8,128)(2,1)S(1)}, bf16[256,1024]{1,0:T(8,128)(2,1)S(1)}, u32[]{:S(2)}, u32[]{:S(2)}) collective-permute-start(bf16[256,1024]{1,0:T(8,128)(2,1)S(1)} %get-tuple-element.59), channel_id=1, source_target_pairs={{0,1},{1,0},{2,3},{3,2},{4,5},{5,4},{6,7},{7,6},{8,9},{9,8},{10,11... | collective-permute-start | bytes 1572872 | tf_op jit(solution)/shard_map/ppermute | solution.py:40
  128.9 14.8 %copy-start.1 = (bf16[512,1024]{1,0:T(8,128)(2,1)S(1)}, bf16[512,1024]{1,0:T(8,128)(2,1)}, u32[]{:S(2)}) copy-start(bf16[512,1024]{1,0:T(8,128)(2,1)} %param.11) | copy-start | bytes 3145732
  129.2 13.4 %collective-permute-start.12 = (bf16[256,1024]{1,0:T(8,128)(2,1)S(1)}, bf16[256,1024]{1,0:T(8,128)(2,1)S(1)}, u32[]{:S(2)}, u32[]{:S(2)}) collective-permute-start(bf16[256,1024]{1,0:T(8,128)(2,1)S(1)} %add_convert_fusion.1), channel_id=1, source_target_pairs={{0,2},{1,3},{2,0},{3,1},{4,6},{5,7},{6,4},{7,5},{8,10},{9,11},{10,... | collective-permute-start | bytes 1572872 | tf_op jit(solution)/shard_map/ppermute | solution.py:40
